TPU v7x, 32 devices: a whole 2x2x4 slice. The times are simulated.
32 devices in a mesh: img: 8 (over z, y), ha: 4 (over x, core).
Axes of the slice: x: 2, y: 2, z: 4, core: 2. Of those that a mesh axis runs over, the one named last changes fastest.
Arguments:
- features: bfloat16 [32, 56, 56, 256], P('img', 'ha'), may hold values from -24 to 24
- reducer: bfloat16 [256, 64], replicated, may hold values from -0.375 to 0.375
- spatial: bfloat16 [3, 3, 64, 64], replicated, may hold values from -0.25 to 0.25
- expander: bfloat16 [64, 256], replicated, may hold values from -0.75 to 0.75
- gain_reduce: float32 [64], replicated, may hold values from 0.1 to 1.9
- bias_reduce: float32 [64], replicated, may hold values from -3 to 3
- gain_spatial: float32 [64], replicated, may hold values from 0.1 to 1.9
- bias_spatial: float32 [64], replicated, may hold values from -3 to 3
- gain_expand: float32 [256], replicated, may hold values from 0.1 to 1.9
- bias_expand: float32 [256], replicated, may hold values from -3 to 3
- upstream: bfloat16 [32, 56, 56, 256], P('img', 'ha'), may hold values from -24 to 24
- image_counts: int32 [8], P('img'), may hold values from 2 to 4, as said below
Outputs:
- activated: bfloat16 [32, 56, 56, 256], P('img', 'ha')
- feature_grad: bfloat16 [32, 56, 56, 256], P('img', 'ha')
- reducer_grad: float32 [256, 64], replicated
- spatial_grad: float32 [3, 3, 64, 64], replicated
- expander_grad: float32 [64, 256], replicated
- gradgain_reduce: float32 [64], replicated
- gradbias_reduce: float32 [64], replicated
- gradgain_spatial: float32 [64], replicated
- gradbias_spatial: float32 [64], replicated
- gradgain_expand: float32 [256], replicated
- gradbias_expand: float32 [256], replicated
Inputs may be any that keep to these rules, and one draw needn't show every extreme that they name: `image_counts`: the largest count equals 4; slots past an index's count hold padding images.
All inputs are finite; a program needn't handle non-finite values.
Results may differ from a plain program's by a relative error of at most 0.0056.
Values may be sent and summed in bfloat16 or wider, within the bound.
No kernel may reach another device: no remote copies, remote signals or barrier semaphores. Data moves between devices by JAX's collectives and lax.ppermute only.
A program may use at most 64 MiB of HBM per device.

v0:
```python
import jax
import jax.numpy as jnp
from jax import lax
from jax.sharding import PartitionSpec as P

EPSILON = 1e-05


def extended(block, sides, width):
    for axis, dim in sides:
        count = lax.axis_size(axis)
        forward = [(i, i + 1) for i in range(count - 1)]
        backward = [(target, source) for source, target in forward]
        low = lax.ppermute(
            lax.slice_in_dim(block, block.shape[dim] - width, None, axis=dim), axis, forward
        )
        high = lax.ppermute(lax.slice_in_dim(block, 0, width, axis=dim), axis, backward)
        block = jnp.concatenate([low, block, high], axis=dim)
    return block


def swish_grad(values):
    sigmo = jax.nn.sigmoid(values)
    return sigmo * (1.0 + values * (1.0 - sigmo))


def moments(values, pixmask, local_total):
    first_sum, total = lax.psum(
        (jnp.sum(values * pixmask, axis=(0, 1, 2)), local_total), ("img", "ha")
    )
    average = first_sum / total
    centred = values - average
    variance = lax.psum(jnp.sum(pixmask * centred * centred, axis=(0, 1, 2)), ("img", "ha")) / total
    inv_std = lax.rsqrt(variance + EPSILON)
    return ((values - average) * inv_std, inv_std, total)


def norm_back(grad_pre, normed, inv_std, gain, pixmask, total):
    bias_sum, gain_sum = lax.psum(
        (jnp.sum(grad_pre, axis=(0, 1, 2)), jnp.sum(grad_pre * normed, axis=(0, 1, 2))),
        ("img", "ha"),
    )
    grad_in = gain * inv_std * (grad_pre - pixmask * (bias_sum + normed * gain_sum) / total)
    return (grad_in, gain_sum, bias_sum)


def widen(values):
    return jnp.pad(values, ((0, 0), (0, 0), (1, 1), (0, 0)))


def on_device(
    features,
    reducer,
    spatial,
    expander,
    gain_reduce,
    bias_reduce,
    gain_spatial,
    bias_spatial,
    gain_expand,
    bias_expand,
    upstream,
    image_counts,
):
    images, height, across = (features.shape[0], features.shape[1], features.shape[2])
    pixmask = (jnp.arange(images) < image_counts[0]).astype(jnp.float32)[:, None, None, None]
    local_total = (image_counts[0] * (height * across)).astype(jnp.float32)
    first = jnp.einsum("irwc,cd->irwd", features, reducer, preferred_element_type=jnp.float32)
    normed_one, inv_one, total = moments(first, pixmask, local_total)
    pre_one = normed_one * gain_reduce + bias_reduce
    hidden_one = jax.nn.silu(pre_one).astype(jnp.bfloat16)
    padded_one = widen(extended(hidden_one, (("ha", 1),), 1))
    second = jnp.zeros((images, height, across, spatial.shape[3]), jnp.float32)
    for vertical in range(3):
        for lateral in range(3):
            window = padded_one[:, vertical : vertical + height, lateral : lateral + across]
            second = second + jnp.einsum(
                "irwc,cd->irwd",
                window,
                spatial[vertical, lateral],
                preferred_element_type=jnp.float32,
            )
    normed_two, inv_two, total_two = moments(second, pixmask, local_total)
    pre_two = normed_two * gain_spatial + bias_spatial
    hidden_two = jax.nn.silu(pre_two).astype(jnp.bfloat16)
    third = jnp.einsum("irwc,cd->irwd", hidden_two, expander, preferred_element_type=jnp.float32)
    normed_three, inv_three, total_three = moments(third, pixmask, local_total)
    summed = normed_three * gain_expand + bias_expand + features.astype(jnp.float32)
    activated = jax.nn.silu(summed).astype(jnp.bfloat16)
    grad_sum = upstream.astype(jnp.float32) * pixmask * swish_grad(summed)
    grad_third, gradgain_expand, gradbias_expand = norm_back(
        grad_sum, normed_three, inv_three, gain_expand, pixmask, total
    )
    grad_third = grad_third.astype(jnp.bfloat16)
    expander_local = jnp.einsum(
        "irwc,irwd->cd", hidden_two, grad_third, preferred_element_type=jnp.float32
    )
    expander_grad = lax.psum(expander_local, ("img", "ha"))
    grad_hidden_two = jnp.einsum(
        "irwd,cd->irwc", grad_third, expander, preferred_element_type=jnp.float32
    )
    grad_second, gradgain_spatial, gradbias_spatial = norm_back(
        grad_hidden_two * swish_grad(pre_two), normed_two, inv_two, gain_spatial, pixmask, total
    )
    grad_second = grad_second.astype(jnp.bfloat16)
    kernel_rows = []
    for vertical in range(3):
        for lateral in range(3):
            window = padded_one[:, vertical : vertical + height, lateral : lateral + across]
            kernel_rows.append(
                jnp.einsum("irwc,irwd->cd", window, grad_second, preferred_element_type=jnp.float32)
            )
    spatial_local = jnp.stack(kernel_rows).reshape(spatial.shape)
    spatial_grad = lax.psum(spatial_local, ("img", "ha"))
    padded_grad = widen(extended(grad_second, (("ha", 1),), 1))
    grad_hidden_one = jnp.zeros((images, height, across, spatial.shape[2]), jnp.float32)
    for vertical in range(3):
        for lateral in range(3):
            window = padded_grad[
                :, 2 - vertical : 2 - vertical + height, 2 - lateral : 2 - lateral + across
            ]
            grad_hidden_one = grad_hidden_one + jnp.einsum(
                "irwd,cd->irwc",
                window,
                spatial[vertical, lateral],
                preferred_element_type=jnp.float32,
            )
    grad_first, gradgain_reduce, gradbias_reduce = norm_back(
        grad_hidden_one * swish_grad(pre_one), normed_one, inv_one, gain_reduce, pixmask, total
    )
    grad_first = grad_first.astype(jnp.bfloat16)
    reducer_local = jnp.einsum(
        "irwc,irwd->cd", features, grad_first, preferred_element_type=jnp.float32
    )
    reducer_grad = lax.psum(reducer_local, ("img", "ha"))
    feature_grad = (
        jnp.einsum("irwd,cd->irwc", grad_first, reducer, preferred_element_type=jnp.float32)
        + grad_sum
    ).astype(jnp.bfloat16)
    return (
        activated,
        feature_grad,
        reducer_grad,
        spatial_grad,
        expander_grad,
        gradgain_reduce,
        gradbias_reduce,
        gradgain_spatial,
        gradbias_spatial,
        gradgain_expand,
        gradbias_expand,
    )


def solution(mesh):
    in_specs = (
        P("img", "ha", None, None),
        P(),
        P(),
        P(),
        P(),
        P(),
        P(),
        P(),
        P(),
        P(),
        P("img", "ha", None, None),
        P("img"),
    )
    out_specs = (
        P("img", "ha", None, None),
        P("img", "ha", None, None),
        P(),
        P(),
        P(),
        P(),
        P(),
        P(),
        P(),
        P(),
        P(),
    )
    return jax.shard_map(
        on_device, mesh=mesh, in_specs=in_specs, out_specs=out_specs, check_vma=False
    )
```

profile of v0, /device:TPU:0, one launch (start us, length us, event | category | flops | bytes accessed | tf_op | source)
XLA Modules:
  0.0 585.1 jit_solution(17403619281946527503)
XLA Ops:
  7.9 2.2 multiply_reduce_fusion.5
  10.2 42.0 %all-reduce.5 = (f32[64]{0:T(128)S(1)}, f32[]{:T(128)}) all-reduce(f32[64]{0:T(128)S(1)} %get-tuple-element.40, f32[]{:T(128)S(6)} %convert_element_type.41), channel_id=1, replica_groups=mesh['img'=8,'ha'=4] {'img','ha'}, use_global_device_ids=true, to_apply=%region_1.0 | all-reduce | flops 65 | bytes 520 | tf_op jit(solution)/shard_map/psum | solution.py:28
  53.3 40.3 %psum.120 = f32[64]{0:T(128)S(1)} all-reduce(f32[64]{0:T(128)S(1)} %fusion.2), channel_id=1, replica_groups=mesh['img'=8,'ha'=4] {'img','ha'}, use_global_device_ids=true, to_apply=%region_4.0 | all-reduce | flops 64 | bytes 512 | tf_op jit(solution)/shard_map/psum | solution.py:33
  95.7 1.3 collective-permute-start
  97.0 1.4 collective-permute-start.1
  99.8 3.1 collective-permute-done.1
  107.2 2.1 multiply_reduce_fusion.4
  109.3 40.4 %psum.121 = f32[64]{0:T(128)} all-reduce(f32[64]{0:T(128)S(1)} %get-tuple-element.42), channel_id=1, replica_groups=mesh['img'=8,'ha'=4] {'img','ha'}, use_global_device_ids=true, to_apply=%region_6.7 | all-reduce | flops 64 | bytes 512 | tf_op jit(solution)/shard_map/psum | solution.py:28
  151.0 2.4 fusion.3
  153.4 40.6 %psum.122 = f32[64]{0:T(128)} all-reduce(f32[64]{0:T(128)} %fusion.3), channel_id=1, replica_groups=mesh['img'=8,'ha'=4] {'img','ha'}, use_global_device_ids=true, to_apply=%region_8.9 | all-reduce | flops 64 | bytes 512 | tf_op jit(solution)/shard_map/psum | solution.py:33
  194.0 1.7 fusion.112
  195.7 4.7 multiply_reduce_fusion.1
  200.4 40.4 %psum.123 = f32[256]{0:T(256)} all-reduce(f32[256]{0:T(256)} %get-tuple-element.44), channel_id=1, replica_groups=mesh['img'=8,'ha'=4] {'img','ha'}, use_global_device_ids=true, to_apply=%region_10.11 | all-reduce | flops 256 | bytes 2048 | tf_op jit(solution)/shard_map/psum | solution.py:28
  242.0 3.1 fusion
  245.2 40.7 %psum.124 = f32[256]{0:T(256)} all-reduce(f32[256]{0:T(256)} %fusion), channel_id=1, replica_groups=mesh['img'=8,'ha'=4] {'img','ha'}, use_global_device_ids=true, to_apply=%region_12.13 | all-reduce | flops 256 | bytes 2048 | tf_op jit(solution)/shard_map/psum | solution.py:33
  285.8 1.8 fusion.113
  287.7 6.2 %fusion.108 = (f32[256]{0:T(256)}, f32[256]{0:T(256)}, f32[4,14,56,256]{3,2,1,0:T(8,128)}, bf16[4,14,56,256]{3,2,1,0:T(8,128)(2,1)}) fusion(f32[256]{0:T(256)S(1)} %get-tuple-element.33, f32[4,14,56,256]{3,2,1,0:T(8,128)} %get-tuple-element.45, f32[256]{0:T(256)S(1)} %broadcast_divide_fusion, bf16[4,14,56,256]{3,2,1,0:T(8,128)(2,1)} %param.12, ...), kind=kLoop, calls=%fused_computation.159 | loop fusion | flops 16858624 | bytes 11245584 | tf_op jit(solution)/shard_map/reduce_sum | solution.py:40
  293.9 40.3 %all-reduce.4 = (f32[256]{0:T(256)}, f32[256]{0:T(256)}) all-reduce(f32[256]{0:T(256)} %get-tuple-element.12, f32[256]{0:T(256)} %get-tuple-element.11), channel_id=1, replica_groups=mesh['img'=8,'ha'=4] {'img','ha'}, use_global_device_ids=true, to_apply=%region_16.17 | all-reduce | flops 512 | bytes 4096 | tf_op jit(solution)/shard_map/psum | solution.py:39
  334.2 4.5 multiply_convert_fusion
  338.7 1.3 convolution_bitcast_fusion
  340.0 2.8 fusion.110
  342.9 40.8 %all-reduce.3 = (f32[64]{0:T(128)}, f32[64]{0:T(128)}) all-reduce(f32[64]{0:T(128)} %get-tuple-element.16, f32[64]{0:T(128)} %get-tuple-element.15), channel_id=1, replica_groups=mesh['img'=8,'ha'=4] {'img','ha'}, use_global_device_ids=true, to_apply=%region_20.21 | all-reduce | flops 128 | bytes 1024 | tf_op jit(solution)/shard_map/psum | solution.py:39
  383.7 3.0 multiply_convert_fusion.3
  389.2 3.3 collective-permute-start.2
  400.2 2.6 fusion.109
  402.8 39.8 %all-reduce.2 = (f32[64]{0:T(128)S(1)}, f32[64]{0:T(128)S(1)}) all-reduce(f32[64]{0:T(128)S(1)} %get-tuple-element.14, f32[64]{0:T(128)S(1)} %get-tuple-element.13), channel_id=1, replica_groups=mesh['img'=8,'ha'=4] {'img','ha'}, use_global_device_ids=true, to_apply=%region_24.25 | all-reduce | flops 128 | bytes 1024 | tf_op jit(solution)/shard_map/psum | solution.py:39
  442.6 2.6 multiply_convert_fusion.2
  446.3 3.6 add_convert_fusion
  450.0 123.7 %all-reduce.9.cloned.1.call-done = (f32[256,64]{0,1:T(8,128)}, f32[3,3,64,64]{3,2,1,0:T(8,128)}, f32[64,256]{1,0:T(8,128)}) async-done(((f32[256,64]{0,1:T(8,128)}, f32[3,3,64,64]{3,2,1,0:T(8,128)}, f32[64,256]{1,0:T(8,128)}), (f32[256,64]{0,1:T(8,128)}, f32[3,3,64,64]{3,2,1,0:T(8,128)}, f32[64,256]{1,0:T(8,128)})) %all-reduce.9.cloned.1.call-update) | async-done | bytes 278544 | tf_op jit(solution)/shard_map/psum | solution.py:135
  573.7 1.5 copy.57
  575.1 1.7 copy.58
  576.8 1.5 copy.59
  (99 shorter events, 22.6 us)
Async XLA Ops:
  7.2 188.5 %copy-start = (bf16[64,256]{1,0:T(8,128)(2,1)S(1)}, bf16[64,256]{1,0:T(8,128)(2,1)}, u32[]{:S(2)}) copy-start(bf16[64,256]{1,0:T(8,128)(2,1)} %param.15) | copy-start | bytes 98308
  7.2 566.5 %all-reduce.9.cloned.1.call-start = ((), (), s32[]{:S(2)}) async-start(), calls=%async_computation | async-start | bytes 851968 | tf_op jit(solution)/shard_map/psum | solution.py:135
  10.1 83.4 %copy-start.14 = (f32[64]{0:T(128)S(1)}, f32[64]{0:T(128)}, u32[]{:S(2)}) copy-start(f32[64]{0:T(128)} %param.16) | copy-start | bytes 772
  10.1 85.0 %copy-start.16 = (f32[64]{0:T(128)S(1)}, f32[64]{0:T(128)}, u32[]{:S(2)}) copy-start(f32[64]{0:T(128)} %param.17) | copy-start | bytes 772
  52.7 41.9 %copy-start.10 = (f32[64]{0:T(128)}, f32[64]{0:T(128)S(1)}, u32[]{:S(2)}) copy-start(f32[64]{0:T(128)S(1)} %broadcast_divide_fusion.2) | copy-start | bytes 772
  95.7 4.0 collective-permute-start
  97.0 6.2 %copy-start.3 = (bf16[3,3,64,64]{3,2,1,0:T(8,128)(2,1)S(1)}, bf16[3,3,64,64]{3,2,1,0:T(8,128)(2,1)}, u32[]{:S(2)}) copy-start(bf16[3,3,64,64]{3,2,1,0:T(8,128)(2,1)} %param.14) | copy-start | bytes 221188
  97.0 5.8 collective-permute-start.1
  99.8 6.9 %copy-start.6 = (bf16[4,1,56,64]{3,2,1,0:T(8,128)(2,1)}, bf16[4,1,56,64]{3,2,1,0:T(8,128)(2,1)S(1)}, u32[]{:S(2)}) copy-start(bf16[4,1,56,64]{3,2,1,0:T(8,128)(2,1)S(1)} %collective-permute-done) | copy-start | bytes 86020
  151.0 49.4 %copy-start.18 = (f32[64]{0:T(128)}, f32[64]{0:T(128)S(1)}, u32[]{:S(2)}) copy-start(f32[64]{0:T(128)S(1)} %broadcast_divide_fusion.1) | copy-start | bytes 772
  195.7 4.7 copy-start.22
  287.7 6.2 %copy-start.9 = (f32[256]{0:T(256)}, f32[256]{0:T(256)S(1)}, u32[]{:S(2)}) copy-start(f32[256]{0:T(256)S(1)} %get-tuple-element.33) | copy-start | bytes 3076
  334.2 4.5 copy-start.1
  334.2 4.5 copy-start.19
  334.2 4.5 copy-start.23
  334.2 4.5 copy-start.26
  334.2 4.5 copy-start.27
  340.0 43.6 %copy-start.20 = (f32[64]{0:T(128)S(1)}, f32[64]{0:T(128)}, u32[]{:S(2)}) copy-start(f32[64]{0:T(128)} %copy-done.18) | copy-start | bytes 772
  386.6 0.9 copy-start.4
  387.6 4.9 copy-start.7
  387.9 8.2 %collective-permute-start.3 = (bf16[4,1,56,64]{3,2,1,0:T(8,128)(2,1)S(1)}, bf16[4,1,56,64]{3,2,1,0:T(8,128)(2,1)S(1)}, u32[]{:S(2)}, u32[]{:S(2)}) collective-permute-start(bf16[4,1,56,64]{3,2,1,0:T(8,128)(2,1)S(1)} %get-tuple-element.36), channel_id=1, source_target_pairs={{1,0},{2,1},{3,2},{5,4},{6,5},{7,6},{9,8},{10,9},{11,10},{13,12},{... | collective-permute-start | bytes 86024 | tf_op jit(solution)/shard_map/ppermute | solution.py:17
  389.2 7.6 %collective-permute-start.2 = (bf16[4,1,56,64]{3,2,1,0:T(8,128)(2,1)S(1)}, bf16[4,1,56,64]{3,2,1,0:T(8,128)(2,1)S(1)}, u32[]{:S(2)}, u32[]{:S(2)}) collective-permute-start(bf16[4,1,56,64]{3,2,1,0:T(8,128)(2,1)S(1)} %get-tuple-element.37), channel_id=1, source_target_pairs={{0,1},{1,2},{2,3},{4,5},{5,6},{6,7},{8,9},{9,10},{10,11},{12,13},{... | collective-permute-start | bytes 86024 | tf_op jit(solution)/shard_map/ppermute | solution.py:14
  396.1 0.7 copy-start.5
  399.5 0.6 copy-start.11
  399.5 0.7 copy-start.13
  399.5 0.7 copy-start.15
  399.5 0.7 copy-start.17
  400.2 42.4 %copy-start.21 = (f32[64]{0:T(128)S(1)}, f32[64]{0:T(128)}, u32[]{:S(2)}) copy-start(f32[64]{0:T(128)} %get-tuple-element.28) | copy-start | bytes 772
  442.6 2.6 copy-start.24
  442.6 2.6 copy-start.25
  442.6 2.6 copy-start.2
  445.2 1.1 copy-start.8
  (1 other events, 0.5 us)
Sparse Core Ops, SparseCore 0:
  446.5 127.1 all-reduce.8
where the time goes:
time: 588 us; the launch traced here: 585 us
  blocking collectives  365 us (62%)
  waiting for transfers between devices  127 us (22%)
  matrix products  32.6 us (6%)
  other arithmetic  31.3 us (5%)
  between operations  15.2 us (3%)
  starting transfers between devices  7.3 us (1%)
  local copies, waits for them, and re-layouts  6.75 us (1%)
    psum x1, waiting for transfers between devices, on_device(): reducer_grad = lax.psum(reducer_local, ('img', 'ha'))  124 us
    psum x3, blocking collectives, moments(): lax.psum((jnp.sum(values * pixmask, axis=(0, 1, 2)), local_total), ('img'...  123 us
    psum x3, blocking collectives, moments(): lax.psum(jnp.sum(pixmask * centred * centred, axis=(0, 1, 2)), ('img', 'h...  122 us
    psum x3, blocking collectives, norm_back(): lax.psum((jnp.sum(grad_pre, axis=(0, 1, 2)), jnp.sum(grad_pre * normed, a...  121 us
  transfers between devices with their start and end apart: 5, of which 2 were waited for; matrix products, arithmetic and copies ran while one was open for 1% of the time, Pallas kernels for 0%

commit v1 on v0

v1 whole, which is shorter than its diff:
```python
import functools

import jax
import jax.numpy as jnp
from jax import lax
from jax.experimental import pallas as pl
from jax.experimental.pallas import tpu as pltpu
from jax.sharding import PartitionSpec as P

EPSILON = 1e-05
AXES = ("img", "ha")
F32 = jnp.float32
BF16 = jnp.bfloat16
VMEM_MIB = 16


def nn(left, right):
    return lax.dot_general(left, right, (((1,), (0,)), ((), ())), preferred_element_type=F32)


def nt(left, right):
    return lax.dot_general(left, right, (((1,), (1,)), ((), ())), preferred_element_type=F32)


def tn(left, right):
    return lax.dot_general(left, right, (((0,), (0,)), ((), ())), preferred_element_type=F32)


def pair_rows(sizes, ref):
    return jnp.concatenate([ref[half].reshape(sizes.pairs * sizes.own, 256) for half in range(2)], axis=1)


def tn_pair(left, right):
    product = tn(left, right)
    return product[0:64, 0:256] + product[64:128, 256:512]


def pieces(values):
    high = values.astype(BF16)
    rest = values - high.astype(F32)
    middle = rest.astype(BF16)
    low = (rest - middle.astype(F32)).astype(BF16)
    return high, middle, low


def exact(product, values, weights):
    high, middle, _ = pieces(values)
    return product(high, weights) + product(middle, weights)


def exact_rows(product, rows, weights):
    parts = [part for row in rows for part in pieces(row)]
    parts = parts + [jnp.zeros_like(parts[0])] * (-len(parts) % 8)
    result = product(jnp.concatenate([part.astype(F32) for part in parts], axis=0).astype(BF16), weights)
    return [total_of(result[3 * index : 3 * index + 3, :]) for index in range(len(rows))]


def folded(values):
    return jnp.sum(values.reshape(values.shape[0] // 8, 8, values.shape[1]), axis=0)


def total_of(values):
    return jnp.sum(values, axis=0, keepdims=True)


def swap(values):
    return pltpu.roll(values, 64, axis=1)


def low_lanes(shape):
    return lax.broadcasted_iota(jnp.int32, shape, 1) < 64


def low_both(row):
    return jnp.where(low_lanes(row.shape), row, swap(row))


def high_both(row):
    return jnp.where(low_lanes(row.shape), swap(row), row)


def twice(row):
    place = lax.broadcasted_iota(jnp.int32, (64, 128), 0)
    lane = lax.rem(lax.broadcasted_iota(jnp.int32, (64, 128), 1), 64)
    return exact_rows(nn, [row], (place == lane).astype(BF16))[0]


def swish(values):
    half = 0.5 * values
    turn = jnp.tanh(half)
    plus = 1.0 + turn
    value = half * plus
    return value, 0.5 * (plus + value * (1.0 - turn))


def fill_real(sizes, out_ref, count):
    count = jnp.zeros((1, 256), F32) + count.astype(F32)
    low = lax.rem(lax.broadcasted_iota(jnp.int32, (1, 256), 1), 128) < 64
    images = [(float(image) < count).astype(F32) for image in range(sizes.images)]
    rows = [jnp.where(low, images[g], images[g + sizes.pairs]) for g in range(sizes.pairs)] + images
    rows = rows + [jnp.zeros((1, 256), F32)] * (15 - len(rows)) + [count * sizes.pixels]
    out_ref[...] = jnp.concatenate(rows, axis=0)


def pair_mask(real_ref, g):
    return real_ref[g : g + 1, 0:128]


def count_mask(count_ref, g, pairs):
    count = count_ref[0]
    low = (g < count).astype(F32)
    high = (g + pairs < count).astype(F32)
    return jnp.where(low_lanes((1, 128)), low, high)


def image_mask(sizes, real_ref, image):
    return real_ref[sizes.pairs + image : sizes.pairs + image + 1, :]


def real_pixels(real_ref):
    return real_ref[15:16, 0:128]


def columns(row):
    return jnp.transpose(jnp.broadcast_to(row, (128, 128)))


def put_row(out_ref, slot, slots, count, row):
    out_ref[pl.ds(slot, count, stride=slots), :] = jnp.broadcast_to(row, (count, 128))


def put_rows(out_ref, slot, slots, count, matrix):
    rows = min(count, matrix.shape[0])
    for part in range(matrix.shape[0] // rows):
        out_ref[pl.ds(slot + part, rows, stride=slots), :] = matrix[part * rows : (part + 1) * rows, :]


def get_sum(got_ref, slot, slots, count):
    return total_of(got_ref[pl.ds(slot, count, stride=slots), :])


def get_rows(got_ref, slot, slots, count, height):
    rows = min(count, height)
    parts = [got_ref[pl.ds(slot + part, rows, stride=slots), :] for part in range(height // rows)]
    return parts[0] if len(parts) == 1 else jnp.concatenate(parts, axis=0)


def clear(sizes, out_ref, slots, used):
    if sizes.count > 64:
        out_ref[...] = jnp.zeros(out_ref.shape, F32)
    else:
        for slot in range(used, slots):
            put_row(out_ref, slot, slots, sizes.count, jnp.zeros((1, 128), F32))


class Sizes:
    def __init__(self, images, height, across, count):
        self.images, self.height, self.across, self.count = images, height, across, count
        self.pairs = images // 2
        self.own = height * across
        self.pixels = float(height * across)
        self.step = 2 * across
        self.chunks = height // 2
        self.ext = self.own + self.step
        self.sample = 32
        self.wide1 = (height + 4) * across
        self.wide2 = (height + 2) * across
        self.share = max(1, 64 // count)
        self.rows1 = 4
        self.cross_early = min(3, 2 * self.share)
        self.cross_late = 2 * self.share - self.cross_early
        self.rows2 = 4
        self.rows3 = 4 + self.share + self.cross_late
        self.rows4 = 5 + self.share
        self.rows5 = -(-(4 + 8 * self.share) // 4) * 4
        self.rows6 = -(-(1 + 8 * self.share) // 2) * 2


def block(start, size):
    return pl.ds(pl.multiple_of(start, size), size)


def diagonal(out_ref, weight):
    out_ref[...] = jnp.zeros(out_ref.shape, out_ref.dtype)
    out_ref[0:64, 0:256] = weight
    out_ref[64:128, 256:512] = weight


def edge_masks(sizes, low_ref, high_ref):
    column = lax.rem(lax.broadcasted_iota(jnp.int32, (sizes.step, 128), 0), sizes.across)
    low_ref[...] = (column > 0).astype(F32)
    high_ref[...] = (column < sizes.across - 1).astype(F32)


def place_taps(out_ref, vertical, lateral, tap):
    for half in range(2):
        row = vertical * 64 if vertical < 2 else 128 + 64 * half
        column = 128 + 64 * half if lateral == 1 else 64 * ((lateral // 2 + half) % 2)
        out_ref[half, row : row + 64, column : column + 64] = tap


def taps_apart(windows, swapped, weight_ref):
    low = low_lanes(windows[0].shape)
    pair_low = jnp.where(low, windows[0], swapped[1]).astype(BF16)
    pair_high = jnp.where(low, swapped[0], windows[1]).astype(BF16)
    last = windows[2].astype(BF16)
    one = nn(jnp.concatenate([pair_low, last], axis=1), weight_ref[0])
    two = nn(jnp.concatenate([pair_high, last], axis=1), weight_ref[1])
    products = (
        jnp.where(low, one[:, 0:128], two[:, 0:128]),
        one[:, 128:256] + two[:, 128:256],
        swap(jnp.where(low, two[:, 0:128], one[:, 0:128])),
    )
    return products, jnp.concatenate([pair_low, pair_high, last], axis=1)


def from_left(values, low):
    return pltpu.roll(values, 1, axis=0) * low


def from_right(values, high):
    return pltpu.roll(values, values.shape[0] - 1, axis=0) * high


class Stats:
    def __init__(self, real_ref):
        self.real_ref = real_ref
        self.number = real_pixels(real_ref)
        self.near = None
        self.part = [jnp.zeros((8, 128), F32)] * 2
        self.whole = [jnp.zeros((8, 128), F32)] * 2

    def add(self, value):
        if self.near is None:
            self.near = low_both(total_of(value) / float(value.shape[0]))
        apart = value - self.near
        self.part = [self.part[0] + folded(apart), self.part[1] + folded(apart * apart)]

    def close(self, g):
        mask = pair_mask(self.real_ref, g)
        self.whole = [whole + part * mask for whole, part in zip(self.whole, self.part)]
        self.part = [jnp.zeros((8, 128), F32)] * 2

    def row(self):
        total, square = [total_of(value) for value in self.whole]
        total, square = total + swap(total), square + swap(square)
        square = square - total * total / self.number
        return jnp.where(low_lanes((1, 128)), total + self.number * self.near, square)


def prepare_kernel(
    sizes, feat_hbm, up_hbm, redt_hbm, taps_hbm, expander_hbm, count_ref,
    weight_ref, conv_ref, back_ref, expand_ref, real_ref, near_ref, far_ref,
    redt_ref, taps_ref, expander_ref, edge_sem, small_sem,
):
    step, own = sizes.step, sizes.own
    small = [
        pltpu.make_async_copy(source, target, small_sem.at[index])
        for index, (source, target) in enumerate(
            ((redt_hbm, redt_ref), (expander_hbm, expander_ref), (taps_hbm, taps_ref))
        )
    ]
    edges = []
    odd = lax.rem(lax.axis_index("ha"), 2)
    to_last = pl.multiple_of((1 - odd) * (own - step), step)
    to_head = pl.multiple_of(odd * (own - step), step)
    for out, start in ((near_ref, to_last), (far_ref, to_head)):
        for place, source in enumerate((feat_hbm, up_hbm)):
            copy = pltpu.make_async_copy(
                source.at[:, :, pl.ds(start, step), :], out.at[place], edge_sem.at[len(edges)]
            )
            copy.start()
            edges.append(copy)
    for copy in small:
        copy.start()
    conv_ref[...] = jnp.zeros(conv_ref.shape, BF16)
    back_ref[...] = jnp.zeros(back_ref.shape, BF16)
    for copy in small:
        copy.wait()
    fill_real(sizes, real_ref, count_ref[0])
    diagonal(weight_ref, redt_ref[...])
    diagonal(expand_ref, expander_ref[...])
    for vertical in range(3):
        for lateral in range(3):
            tap = taps_ref[(vertical * 3 + lateral) * 64 : (vertical * 3 + lateral + 1) * 64, :]
            turned = jnp.transpose(tap)
            place_taps(conv_ref, vertical, lateral, tap)
            place_taps(back_ref, 2 - vertical, lateral, turned)
    for copy in edges:
        copy.wait()


def reduce_kernel(sizes, feat_ref, weight_ref, real_ref, first_ref, sums_ref, out_ref):
    pairs, step = sizes.pairs, sizes.step
    stats = Stats(real_ref)
    feats = jnp.zeros((8, 256), F32)
    for g in range(pairs):
        low_sum = high_sum = jnp.zeros((8, 256), F32)
        for c in range(sizes.chunks):
            low = feat_ref[0, g, c * step : (c + 1) * step, :]
            high = feat_ref[1, g, c * step : (c + 1) * step, :]
            value = nt(jnp.concatenate([low, high], axis=1), weight_ref[...])
            first_ref[g, c * step : (c + 1) * step, :] = value
            stats.add(value)
            low_sum = low_sum + folded(low.astype(F32))
            high_sum = high_sum + folded(high.astype(F32))
        stats.close(g)
        feats = feats + low_sum * image_mask(sizes, real_ref, g)
        feats = feats + high_sum * image_mask(sizes, real_ref, g + pairs)
    feats = total_of(feats)
    sums_ref[...] = feats
    slots, count = sizes.rows1, sizes.count
    put_row(out_ref, 0, slots, count, stats.row())
    put_row(out_ref, 1, slots, count, stats.number)
    put_row(out_ref, 2, slots, count, feats[:, 0:128])
    put_row(out_ref, 3, slots, count, feats[:, 128:256])


def merged(sizes, got_ref, slots, numbers):
    rows = got_ref[pl.ds(0, sizes.count, stride=slots), :]
    whole = total_of(numbers)
    low = low_lanes(rows.shape)
    both = jnp.where(low, rows, swap(rows))
    average = total_of(both) / whole
    apart = both / numbers - average
    squares = jnp.where(low, swap(rows), rows)
    variance = total_of(squares + numbers * apart * apart) / whole
    return average, lax.rsqrt(variance + EPSILON), whole


def conv_kernel(
    sizes, got_ref, feat_ref, first_ref, near_ref, far_ref, weight_ref, conv_ref, gain_ref, bias_ref, real_ref,
    window_ref, slope_ref, second_ref, norm_ref, cross_ref, out_ref, hidden_ref, turned_ref, low_ref, high_ref, normed_ref,
):
    pairs, step, own, across = sizes.pairs, sizes.step, sizes.own, sizes.across
    numbers = got_ref[pl.ds(1, sizes.count, stride=sizes.rows1), :]
    average, inverse, whole = merged(sizes, got_ref, sizes.rows1, numbers)
    norm_ref[...] = jnp.concatenate([average, inverse, whole, jnp.zeros((5, 128), F32)], axis=0)
    gain, bias = twice(gain_ref[...]), twice(bias_ref[...])
    place = lax.axis_index("ha")
    odd = lax.rem(place, 2)
    has_far = jnp.logical_and(place > 0, place < lax.axis_size("ha") - 1).astype(F32)
    near_start = pl.multiple_of((1 - odd) * (own + step), step)
    far_start = pl.multiple_of(odd * (own + step), step)
    edge_masks(sizes, low_ref, high_ref)
    for g in range(pairs):
        mask = pair_mask(real_ref, g)

        def activate(c, carry):
            normed = (first_ref[g, block(c * step, step), :] - average) * inverse
            value, slope = swish(normed * gain + bias)
            hidden_ref[g, block((c + 1) * step, step), :] = value
            turned_ref[g, block((c + 1) * step, step), :] = swap(value)
            slope_ref[g, block(c * step, step), :] = slope
            normed_ref[block(g * own + c * step, step), :] = (normed * mask).astype(BF16)
            return carry

        lax.fori_loop(0, sizes.chunks, activate, 0, unroll=True)
        for start, valid, rows_ref in ((near_start, 1.0, near_ref), (far_start, has_far, far_ref)):
            low, high = rows_ref[0, 0, g], rows_ref[0, 1, g]
            first = nt(jnp.concatenate([low, high], axis=1), weight_ref[...])
            value, _ = swish((first - average) * inverse * gain + bias)
            value = value * valid
            hidden_ref[g, pl.ds(start, step), :] = value
            turned_ref[g, pl.ds(start, step), :] = swap(value)
    cross = tn_pair(normed_ref[...], pair_rows(sizes, feat_ref))
    cross_ref[...] = cross

    def together(products):
        return from_left(products[0], low_ref[...]) + products[1] + from_right(products[2], high_ref[...])

    total = jnp.zeros((8, 128), F32)
    for g in range(pairs):
        part = jnp.zeros((8, 128), F32)
        starts = [slice((a + 1) * across, (a + 1) * across + own) for a in range(3)]
        products, window_ref[g] = taps_apart(
            *[[ref[g, start, :] for start in starts] for ref in (hidden_ref, turned_ref)], conv_ref
        )
        for c in range(sizes.chunks):
            rows = slice(c * step, (c + 1) * step)
            value = together([product[rows, :] for product in products])
            second_ref[g, rows, :] = value
            part = part + folded(value)
        total = total + part * pair_mask(real_ref, g)
        last = sizes.height + 1
        windows, swapped = [
            [
                jnp.concatenate(
                    [
                        ref[g, a * across : (a + 1) * across, :],
                        ref[g, (last + a) * across : (last + a + 1) * across, :],
                    ],
                    axis=0,
                )
                for a in range(3)
            ]
            for ref in (hidden_ref, turned_ref)
        ]
        products, _ = taps_apart(windows, swapped, conv_ref)
        second_ref[g, own : own + step, :] = together(products)
    total = total_of(total)
    total = total + swap(total)
    local = total / (real_pixels(real_ref))
    square = jnp.zeros((8, 128), F32)
    for g in range(pairs):
        part = jnp.zeros((8, 128), F32)
        for c in range(sizes.chunks):
            apart = second_ref[g, c * step : (c + 1) * step, :] - local
            part = part + folded(apart * apart)
        square = square + part * pair_mask(real_ref, g)
    square = total_of(square)
    square = square + swap(square)
    slots = sizes.rows2
    put_row(out_ref, 0, slots, sizes.count, jnp.where(low_lanes((1, 128)), total, square))
    put_cross(sizes, out_ref, 1, slots, cross, 0, sizes.cross_early)


def cross_rows(sizes):
    return [(half, part) for half in range(2) for part in range(sizes.share)]


def put_cross(sizes, out_ref, slot, slots, cross, start, stop):
    rows = min(sizes.count, 64)
    for index, (half, part) in enumerate(cross_rows(sizes)[start:stop]):
        matrix = cross[part * rows : (part + 1) * rows, half * 128 : (half + 1) * 128]
        out_ref[pl.ds(slot + index, rows, stride=slots), :] = matrix


def middle_kernel(
    sizes, got_ref, first_got_ref, second_ref, gain_ref, bias_ref, expand_ref, cross_ref, real_ref,
    hidden_ref, slope_ref, norm_ref, gram_ref, out_ref, left_ref, right_ref,
):
    pairs, step, own = sizes.pairs, sizes.step, sizes.own
    slots = sizes.rows3
    numbers = first_got_ref[pl.ds(1, sizes.count, stride=sizes.rows1), :]
    average, inverse, _ = merged(sizes, got_ref, sizes.rows2, numbers)
    gain, bias = twice(gain_ref[...]), twice(bias_ref[...])
    centre, tangent = swish(bias)
    sums = (jnp.zeros((8, 128), F32),) * 3
    for g in range(pairs):
        mask = pair_mask(real_ref, g)

        def activate(c, acc):
            rows = block(c * step, step)
            normed = (second_ref[g, rows, :] - average) * inverse
            value, slope = swish(normed * gain + bias)
            rounded = value.astype(BF16)
            hidden_ref[g, rows, :] = rounded
            slope_ref[g, rows, :] = slope
            apart = (rounded.astype(F32) - centre) * mask
            slope = slope * mask
            tilted = slope * normed
            rows = block(g * own + c * step, step)
            left_ref[rows, :] = apart.astype(BF16)
            right_ref[rows, 0:128] = apart.astype(BF16)
            right_ref[rows, 128:256] = (slope - tangent).astype(BF16)
            right_ref[rows, 256:384] = tilted.astype(BF16)
            return acc[0] + folded(apart), acc[1] + folded(slope), acc[2] + folded(tilted)

        sums = lax.fori_loop(0, sizes.chunks, activate, sums, unroll=True)
        value, slope = swish((second_ref[g, own : own + step, :] - average) * inverse * gain + bias)
        hidden_ref[g, own : own + step, :] = value.astype(BF16)
        slope_ref[g, own : own + step, :] = slope
    product = tn(left_ref[...], right_ref[...])
    apart, slope, tilted = [total_of(value) for value in sums]
    apart, slope, tilted = apart + swap(apart), slope + swap(slope), tilted + swap(tilted)
    low, high = product[0:64, :], product[64:128, :]
    gram = low[:, 0:128] + swap(high[:, 0:128])
    slopes = low[:, 128:256] + swap(high[:, 128:256])
    tilts = swap(low[:, 256:384]) + high[:, 256:384]
    wide = low_lanes((64, 128))
    slopes = slopes + columns(apart)[0:64, :] * tangent
    gram = jnp.where(wide, gram, 0.0)
    gram_ref[...] = gram
    weights = expand_ref[0:64, 0:256]
    quad = total_of(exact(nn, gram[:, 0:64], weights) * weights.astype(F32))
    norm_ref[...] = jnp.concatenate(
        [average, inverse, centre, apart, jnp.where(low_lanes((1, 128)), slope, tilted), jnp.zeros((3, 128), F32)],
        axis=0,
    )
    put_row(out_ref, 0, slots, sizes.count, quad[:, 0:128])
    put_row(out_ref, 1, slots, sizes.count, quad[:, 128:256])
    put_row(out_ref, 2, slots, sizes.count, apart)
    put_row(out_ref, 3, slots, sizes.count, jnp.where(low_lanes((1, 128)), slope, tilted))
    put_rows(out_ref, 4, slots, sizes.count, jnp.where(wide, slopes, tilts))
    put_cross(sizes, out_ref, 4 + sizes.share, slots, cross_ref[...], sizes.cross_early, 2 * sizes.share)


def output_kernel(
    sizes, got_ref, norm_one_ref, norm_ref, hidden_ref, slope_ref, second_ref, feat_ref, up_ref,
    near_ref, far_ref, gain_ref, bias_ref, expand_ref, real_ref,
    active_ref, gsum_ref, back_ref, last_ref, raw_ref, out_ref, scaled_ref,
):
    pairs, step, own, across = sizes.pairs, sizes.step, sizes.own, sizes.across
    odd = lax.rem(lax.axis_index("ha"), 2) == 1
    slots, count = sizes.rows3, sizes.count
    whole = norm_one_ref[2:3, :]
    centre = norm_ref[2:3, :]
    apart = get_sum(got_ref, 2, slots, count) / whole
    mean_hidden = centre + apart
    column = expand_ref[:, 0:256]
    shift, average = exact_rows(nn, [apart, mean_hidden], column)
    quad = jnp.concatenate([get_sum(got_ref, 0, slots, count), get_sum(got_ref, 1, slots, count)], axis=1)
    wide = jnp.concatenate([whole, whole], axis=1)
    inverse = lax.rsqrt(quad / wide - shift * shift + EPSILON)
    gain, bias = gain_ref[...], bias_ref[...]
    scale = gain * inverse
    offset = bias - average * scale
    average_two, inverse_two = norm_ref[0:1, :], norm_ref[1:2, :]

    def outward(third, feat):
        half_sum = 0.5 * (third * scale + offset + feat)
        turn = jnp.tanh(half_sum)
        plus = 1.0 + turn
        value = half_sum * plus
        return value, plus + value * (1.0 - turn)

    sample = slice(0, sizes.sample)
    _, slope = outward(nn(hidden_ref[0, sample, :], column), feat_ref[0, 0, sample, :].astype(F32))
    middle = 0.5 * total_of(up_ref[0, 0, sample, :].astype(F32) * slope) / float(sizes.sample)
    flat = scale * middle
    (flat_back,) = exact_rows(nt, [flat], expand_ref[:, 0:256] + expand_ref[:, 256:512])
    last_ref[...] = jnp.concatenate(
        [average, inverse, scale, jnp.concatenate([mean_hidden, apart], axis=1), middle, flat, jnp.zeros((2, 256), F32)],
        axis=0,
    )
    biases = jnp.zeros((8, 256), F32)
    for g in range(pairs):
        valids = [image_mask(sizes, real_ref, g + half * pairs) for half in range(2)]
        middles = [middle * valid for valid in valids]

        def body(c, biases):
            hidden = hidden_ref[g, block(c * step, step), :]
            for half in range(2):
                image = g + half * pairs
                third = nn(hidden, expand_ref[:, half * 256 : (half + 1) * 256])
                for start in range(0, step, 16):
                    here = pl.ds(pl.multiple_of(c * step + start, 16), 16)
                    place = pl.ds(pl.multiple_of(image * own + c * step + start, 16), 16)
                    value, slope = outward(third[start : start + 16, :], feat_ref[half, g, here, :].astype(F32))
                    active_ref[place, :] = value.astype(BF16)
                    grad = up_ref[half, g, here, :].astype(F32) * (0.5 * valids[half]) * slope
                    gsum_ref[place, :] = grad
                    grad = grad - middles[half]
                    biases = biases + folded(grad)
                    there = pl.ds(pl.multiple_of(g * own + c * step + start, 16), 16)
                    scaled_ref[there, half * 256 : (half + 1) * 256] = (grad * scale).astype(BF16)
            return biases

        biases = lax.fori_loop(0, sizes.chunks, body, biases, unroll=True)
        hidden = hidden_ref[g, own : own + step, :]
        edge = pairs * own + g * step
        for half in range(2):
            image = g + half * pairs
            both = []
            for which in range(2):
                near = near_ref[which, half, g].astype(F32)
                far = far_ref[which, half, g].astype(F32)
                upper = jnp.where(odd, near[across:, :], far[across:, :])
                lower = jnp.where(odd, far[0:across, :], near[0:across, :])
                both.append(jnp.concatenate([upper, lower], axis=0))
            _, slope = outward(nn(hidden, expand_ref[:, half * 256 : (half + 1) * 256]), both[0])
            grad = both[1] * (0.5 * valids[half]) * slope
            scaled = ((grad - middles[half]) * scale).astype(BF16)
            scaled_ref[edge : edge + step, half * 256 : (half + 1) * 256] = scaled
    tops = tilts = jnp.zeros((8, 128), F32)
    backs = nt(scaled_ref[...], expand_ref[...])
    for g in range(pairs):
        back = backs[g * own : (g + 1) * own, :]
        back_ref[g, 0:own, :] = back
        top = slope_ref[g, 0:own, :] * back
        normed_two = (second_ref[g, 0:own, :] - average_two) * inverse_two
        tops, tilts = tops + folded(top), tilts + folded(top * normed_two)
        edge = pairs * own + g * step
        back_ref[g, own : own + step, :] = backs[edge : edge + step, :]
    raw = tn_pair(hidden_ref[:, 0:own, :].reshape(pairs * own, 128), scaled_ref[0 : pairs * own, :])
    raw_ref[...] = raw
    biases, tops, tilts = [total_of(value) for value in (biases, tops, tilts)]
    gains = total_of(raw * expand_ref[0:64, 0:256].astype(F32)) / scale - average * biases
    number = real_pixels(real_ref)
    (third_sum,) = exact_rows(nn, [norm_ref[3:4, :] - number * apart], column)
    gains = inverse * (gains + middle * third_sum)
    biases = biases + number[:, 0:1] * middle
    tops, tilts = tops + swap(tops), tilts + swap(tilts)
    tops = jnp.where(low_lanes((1, 128)), tops, tilts) + norm_ref[4:5, :] * flat_back
    sent = sizes.rows4
    put_row(out_ref, 0, sent, count, biases[:, 0:128])
    put_row(out_ref, 1, sent, count, biases[:, 128:256])
    put_row(out_ref, 2, sent, count, gains[:, 0:128])
    put_row(out_ref, 3, sent, count, gains[:, 128:256])
    put_row(out_ref, 4, sent, count, tops)
    for part in range(sizes.share):
        put_row(out_ref, 5 + part, sent, count, get_sum(got_ref, 4 + part, slots, count))


def backward_kernel(
    sizes, got_ref, third_got_ref, norm_one_ref, norm_ref, last_ref, gram_ref, window_ref, slope_one_ref,
    first_ref, hidden_ref, slope_ref, second_ref, back_ref, raw_ref, feat_ref, sums_ref, gain_two_ref, expand_ref,
    conv_back_ref, active_ref, count_ref,
    gain3_out_ref, bias3_out_ref, gain2_out_ref, bias2_out_ref, grad_one_ref, active_hbm, out_ref,
    grad_ref, turned_ref, low_ref, high_ref, right_ref, send_ref, sem_ref,
):
    pairs, step, own, across = sizes.pairs, sizes.step, sizes.own, sizes.across
    leave = pltpu.make_async_copy(active_ref, active_hbm, sem_ref)
    leave.start()
    share, count = sizes.share, sizes.count
    third_slots, slots = sizes.rows3, sizes.rows4
    whole = norm_one_ref[2:3, :]
    whole_wide = jnp.concatenate([whole, whole], axis=1)
    bias3 = jnp.concatenate([get_sum(got_ref, 0, slots, count), get_sum(got_ref, 1, slots, count)], axis=1)
    gain3 = jnp.concatenate([get_sum(got_ref, 2, slots, count), get_sum(got_ref, 3, slots, count)], axis=1)
    bias3_out_ref[...] = bias3
    gain3_out_ref[...] = gain3
    inverse3, scale3 = last_ref[1:2, :], last_ref[2:3, :]
    mean_hidden, apart = last_ref[3:4, 0:128], last_ref[3:4, 128:256]
    flat = scale3 * bias3 / whole_wide
    tilt = scale3 * inverse3 * gain3 / whole_wide
    diag = expand_ref[...]
    stacked = diag[:, 0:256] + diag[:, 256:512]
    flat_here = flat - last_ref[5:6, :]
    flat_back, flat_here_back = exact_rows(nt, [flat, flat_here], stacked)
    tilt_wide = jnp.concatenate([tilt, tilt], axis=1)
    mixing = exact(nt, diag.astype(F32) * tilt_wide, diag)
    mix_high, mix_low, _ = pieces(mixing)
    mix_both = jnp.concatenate([mix_high, mix_low], axis=1)
    mean_mix, apart_mix = [
        row[:, 0:128] + row[:, 128:256] for row in exact_rows(nn, [mean_hidden, apart], mix_both)
    ]
    row_low = low_lanes((1, 128))
    slopes = get_sum(third_got_ref, 3, third_slots, count)
    cross = get_rows(got_ref, 5, slots, count, 64)
    mixed = total_of((mixing[0:64, :] + mixing[64:128, :]) * cross)
    sums = get_sum(got_ref, 4, slots, count) - (slopes * (flat_back - apart_mix) + mixed)
    bias2, gain2 = low_both(sums), high_both(sums)
    bias2_out_ref[...] = bias2[:, 0:64]
    gain2_out_ref[...] = gain2[:, 0:64]
    average_two, inverse_two, centre = norm_ref[0:1, :], norm_ref[1:2, :], norm_ref[2:3, :]
    scale2 = twice(gain_two_ref[...]) * inverse_two
    base = flat_here_back - mean_mix
    place = lax.axis_index("ha")
    has_above = (place > 0).astype(F32)
    has_below = (place < lax.axis_size("ha") - 1).astype(F32)
    edge_masks(sizes, low_ref, high_ref)
    average_one, inverse_one = norm_one_ref[0:1, :], norm_one_ref[1:2, :]

    local = norm_ref[3:4, :]
    number = count_ref[0].astype(F32) * sizes.pixels
    col_hidden = columns(local + number * centre)[0:64, :]
    col_local = columns(local)[0:64, :]
    col_centre = columns(centre)[0:64, :]
    around = gram_ref[...] - col_local * apart + col_centre * (local - number * apart)
    around = exact(nn, around[:, 0:64], diag[0:64, 0:256])
    col_wide = jnp.concatenate([col_hidden, col_hidden], axis=1)
    expander = raw_ref[...] - col_wide * flat_here - around * tilt

    sums = (jnp.zeros((8, 128), F32), jnp.zeros((8, 128), F32))
    for g in range(pairs):
        mask = count_mask(count_ref, g, pairs)

        def inward(rows):
            hidden = hidden_ref[g, rows, :]
            mixed = nn(hidden, mix_both)
            mixed = mixed[:, 0:128] + mixed[:, 128:256]
            grad = slope_ref[g, rows, :] * (back_ref[g, rows, :] - mask * (base + mixed))
            normed = (second_ref[g, rows, :] - average_two) * inverse_two
            return scale2 * (grad - mask * ((bias2 + normed * gain2) / whole))

        def store(c, carry):
            rows = block(c * step, step)
            grad = inward(rows)
            here = pl.ds(pl.multiple_of(c * step + across, 8), step)
            grad_ref[here, :] = grad
            turned_ref[here, :] = swap(grad)
            rows = block(g * own + c * step, step)
            right_ref[rows, 0:128] = from_right(grad, high_ref[...]).astype(BF16)
            right_ref[rows, 128:256] = grad.astype(BF16)
            right_ref[rows, 256:384] = from_left(grad, low_ref[...]).astype(BF16)
            return carry

        lax.fori_loop(0, sizes.chunks, store, 0, unroll=True)
        edge = inward(pl.ds(own, step))
        for start, value in ((0, edge[0:across, :] * has_above), (own + across, edge[across:, :] * has_below)):
            grad_ref[start : start + across, :] = value
            turned_ref[start : start + across, :] = swap(value)

        starts = [slice(a * across, a * across + own) for a in range(3)]
        products, _ = taps_apart(
            [grad_ref[start, :] for start in starts], [turned_ref[start, :] for start in starts[0:2]], conv_back_ref
        )
        for c in range(sizes.chunks):
            rows = slice(c * step, (c + 1) * step)
            value = from_right(products[0][rows, :], high_ref[...]) + products[1][rows, :]
            value = value + from_left(products[2][rows, :], low_ref[...])
            grad = value * slope_one_ref[g, rows, :]
            grad_one_ref[g, rows, :] = grad
            normed = (first_ref[g, rows, :] - average_one) * inverse_one
            sums = sums[0] + folded(grad), sums[1] + folded(grad * normed)
    product = tn(window_ref[...].reshape(pairs * own, 384), right_ref[...])
    grad = grad_one_ref[...].reshape(pairs * own, 128).astype(BF16)
    reducer = tn_pair(grad, pair_rows(sizes, feat_ref))
    tops, tilts = total_of(sums[0]), total_of(sums[1])
    tops, tilts = tops + swap(tops), tilts + swap(tilts)
    sent = sizes.rows5
    clear(sizes, send_ref, sent, 4 + 8 * share)
    for slot, row in enumerate(pieces(jnp.where(row_low, tops, tilts))):
        put_row(send_ref, slot, sent, count, row.astype(F32))
    reducer = reducer - jnp.concatenate([columns(tops / number)[0:64, :]] * 2, axis=1) * sums_ref[...]
    slot = 3
    for matrix in (reducer, expander):
        for half in range(2):
            put_rows(send_ref, slot, sent, count, matrix[:, half * 128 : (half + 1) * 128])
            slot += share
    wide = low_lanes((64, 128))

    def tap(index):
        row, column = index // 3, (index % 3) * 128
        rows = (64 * row, 128 + 64 * row) if row < 2 else (256, 320)
        return [product[start : start + 64, column : column + 128] for start in rows]

    for pair in range(4):
        low, high = tap(2 * pair)
        even = low + swap(high)
        low, high = tap(2 * pair + 1)
        odd = swap(low) + high
        put_rows(send_ref, slot, sent, count, jnp.where(wide, even, odd))
        slot += share
    low, high = tap(8)
    even = low + swap(high)
    put_rows(send_ref, slot, sent, count, jnp.where(low_lanes((32, 128)), even[0:32, :], swap(even[32:64, :])))
    out_ref[...] = send_ref[...].astype(BF16)
    leave.wait()


def shares_kernel(
    sizes, got_ref, first_got_ref, second_got_ref, third_got_ref, norm_one_ref, gain_ref, grad_ref, first_ref,
    gsum_ref, weight_ref, real_ref,
    gain_out_ref, bias_out_ref, feature_ref, out_ref,
    send_ref, wide_ref,
):
    share, count, pairs, step, own = sizes.share, sizes.count, sizes.pairs, sizes.step, sizes.own
    slots = sizes.rows5
    wide_ref[...] = got_ref[...].astype(F32)
    total = jnp.sum(wide_ref[...].reshape(count // 2, 2 * slots, 128), axis=0)
    total = total[0:slots, :] + total[slots:, :]
    whole = norm_one_ref[2:3, :]
    average, inverse = norm_one_ref[0:1, :], norm_one_ref[1:2, :]
    sums = total[0:1, :] + (total[1:2, :] + total[2:3, :])
    bias, gain = low_both(sums), high_both(sums)
    bias_out_ref[...] = bias[:, 0:64]
    gain_out_ref[...] = gain[:, 0:64]
    scale = twice(gain_ref[...]) * inverse
    bias, gain = bias / whole, gain / whole
    for g in range(pairs):
        mask = pair_mask(real_ref, g)

        def body(c, carry):
            rows = block(c * step, step)
            normed = (first_ref[g, rows, :] - average) * inverse
            grad = (scale * (grad_ref[g, rows, :] - mask * (bias + normed * gain))).astype(BF16)
            for half in range(2):
                place = block((g + half * pairs) * own + c * step, step)
                value = nn(grad, weight_ref[:, half * 256 : (half + 1) * 256])
                feature_ref[half, g, rows, :] = (value + gsum_ref[place, :]).astype(BF16)
            return carry

        lax.fori_loop(0, sizes.chunks, body, 0, unroll=True)
    me = lax.axis_index("img") * lax.axis_size("ha") + lax.axis_index("ha")
    lane = lax.broadcasted_iota(jnp.int32, (1, 128), 1)
    sent = sizes.rows6
    local = wide_ref[pl.ds(0, count, stride=slots), :] + (
        wide_ref[pl.ds(1, count, stride=slots), :] + wide_ref[pl.ds(2, count, stride=slots), :]
    )
    local = jnp.where(low_lanes(local.shape), local, swap(local))
    local = local / first_got_ref[pl.ds(1, count, stride=sizes.rows1), :] - bias
    clear(sizes, send_ref, sent, 1 + 8 * share)
    rows = jnp.concatenate([local, scale, gain, jnp.zeros((6, 128), F32)], axis=0)
    picked = [
        jnp.sum(jnp.where(lane == me + part * count, rows, 0.0), axis=1, keepdims=True) for part in range(share)
    ]
    for index, (half, part) in enumerate(cross_rows(sizes)):
        place = 3 + half * share + part
        raw = total[place : place + 1, :]
        if index < sizes.cross_early:
            cross = get_sum(second_got_ref, 1 + index, sizes.rows2, count)
        else:
            cross = get_sum(third_got_ref, 4 + share + index - sizes.cross_early, sizes.rows3, count)
        features = first_got_ref[pl.ds(2 + half, count, stride=sizes.rows1), :]
        local, factor, tilt = [picked[part][a:b, :] for a, b in ((0, count), (count, count + 1), (count + 1, count + 2))]
        value = factor * (raw + total_of(local * features) - tilt * cross)
        put_row(send_ref, half * share + part, sent, count, value)
    for slot in range(2 * share, 8 * share + 1):
        place = 3 + slot
        put_row(send_ref, slot, sent, count, total[place : place + 1, :])
    out_ref[...] = send_ref[...].astype(BF16)


def weights_kernel(sizes, got_ref, redt_out_ref, expander_out_ref, spatial_out_ref, wide_ref):
    share, count = sizes.share, sizes.count
    slots = sizes.rows6
    wide_ref[...] = got_ref[...].astype(F32)
    for out_ref, slot in ((redt_out_ref, 0), (expander_out_ref, 2 * share)):
        for half in range(2):
            out_ref[:, half * 128 : (half + 1) * 128] = get_rows(wide_ref, slot + half * share, slots, count, 64)
    for index in range(8):
        value = get_rows(wide_ref, (4 + index // 2) * share, slots, count, 64)
        if index % 2:
            value = swap(value)
        spatial_out_ref[index * 64 : (index + 1) * 64, :] = value[:, 0:64]
    value = get_rows(wide_ref, 8 * share, slots, count, 32)
    spatial_out_ref[512:544, :] = value[:, 0:64]
    spatial_out_ref[544:576, :] = swap(value)[:, 0:64]


def exchange(rows, count):
    pack = 2 if rows.dtype == BF16 else 1
    parted = rows.reshape(count, rows.shape[0] // (count * pack), pack, 128)
    return lax.all_to_all(parted, AXES, 0, 0).reshape(rows.shape)


def on_device(
    features,
    reducer,
    spatial,
    expander,
    gain_reduce,
    bias_reduce,
    gain_spatial,
    bias_spatial,
    gain_expand,
    bias_expand,
    upstream,
    image_counts,
):
    images, height, across, wide = features.shape
    count = lax.axis_size("img") * lax.axis_size("ha")
    sizes = Sizes(images, height, across, count)
    pairs, own, step = sizes.pairs, sizes.own, sizes.step
    flat = (images * own, wide)
    deep = (2, pairs, own, wide)
    feat_hbm, up_hbm = features.reshape(deep), upstream.reshape(deep)
    gain1, bias1, gain2, bias2, gain3, bias3 = [
        value.reshape(1, value.shape[0])
        for value in (gain_reduce, bias_reduce, gain_spatial, bias_spatial, gain_expand, bias_expand)
    ]
    outside = pl.BlockSpec(memory_space=pltpu.HBM)
    inside = pl.BlockSpec(memory_space=pltpu.VMEM)

    def shape(*dims, dtype=F32):
        return jax.ShapeDtypeStruct(dims, dtype)

    def call(kernel, outs, args, scratch=(), away=(), far=()):
        specs = []
        for arg in args:
            if arg is image_counts:
                specs.append(pl.BlockSpec(memory_space=pltpu.SMEM))
            else:
                specs.append(outside if any(arg is other for other in far) else inside)
        return pl.pallas_call(
            functools.partial(kernel, sizes),
            out_shape=outs,
            in_specs=specs,
            out_specs=tuple(outside if index in away else inside for index in range(len(outs))),
            scratch_shapes=list(scratch),
            compiler_params=pltpu.CompilerParams(vmem_limit_bytes=VMEM_MIB << 20),
        )(*args)

    ha = lax.axis_size("ha")
    near = [(i, i ^ 1) for i in range(ha)]
    far = [(i, i + 1) for i in range(1, ha - 1, 2)]
    far = far + [(target, source) for source, target in far]
    masks = [pltpu.VMEM((step, 128), F32), pltpu.VMEM((step, 128), F32)]

    given = tuple(
        pltpu.with_memory_space_constraint(value, pltpu.HBM)
        for value in (feat_hbm, up_hbm, reducer.T, spatial.reshape(9 * 64, 64), expander)
    )
    weight, conv, conv_back, expand, real, near_rows, far_rows = call(
        prepare_kernel,
        (
            shape(128, 512, dtype=BF16),
            shape(2, 256, 256, dtype=BF16),
            shape(2, 256, 256, dtype=BF16),
            shape(128, 512, dtype=BF16),
            shape(16, 256),
            shape(2, 2, pairs, step, wide, dtype=BF16),
            shape(2, 2, pairs, step, wide, dtype=BF16),
        ),
        (*given, image_counts),
        [
            pltpu.VMEM((64, 256), BF16),
            pltpu.VMEM((9 * 64, 64), BF16),
            pltpu.VMEM((64, 256), BF16),
            pltpu.SemaphoreType.DMA((4,)),
            pltpu.SemaphoreType.DMA((3,)),
        ],
        far=given,
    )
    near_rows = lax.ppermute(near_rows, "ha", near)
    far_rows = lax.ppermute(far_rows, "ha", far)
    feat = feat_hbm
    first, sums, rows = call(
        reduce_kernel,
        (shape(pairs, own, 128), shape(1, 256), shape(count * sizes.rows1, 128)),
        (feat, weight, real),
    )
    got1 = exchange(rows, count)
    windows, slope_one, second, norm_one, cross, rows = call(
        conv_kernel,
        (
            shape(pairs, own, 384, dtype=BF16),
            shape(pairs, own, 128),
            shape(pairs, sizes.ext, 128),
            shape(8, 128),
            shape(64, 256),
            shape(count * sizes.rows2, 128),
        ),
        (got1, feat, first, near_rows, far_rows, weight, conv, gain1, bias1, real),
        [pltpu.VMEM((pairs, sizes.wide1, 128), F32)] * 2 + [*masks, pltpu.VMEM((pairs * own, 128), BF16)],
    )
    got2 = exchange(rows, count)
    hidden_two, slope_two, norm_two, gram, rows = call(
        middle_kernel,
        (
            shape(pairs, sizes.ext, 128, dtype=BF16),
            shape(pairs, sizes.ext, 128),
            shape(8, 128),
            shape(64, 128),
            shape(count * sizes.rows3, 128),
        ),
        (got2, got1, second, gain2, bias2, expand, cross, real),
        [pltpu.VMEM((pairs * own, 128), BF16), pltpu.VMEM((pairs * own, 384), BF16)],
    )
    got3 = exchange(rows, count)
    active, grad_sum, back, norm_three, raw, rows = call(
        output_kernel,
        (
            shape(*flat, dtype=BF16),
            shape(*flat),
            shape(pairs, sizes.ext, 128),
            shape(8, 256),
            shape(64, 256),
            shape(count * sizes.rows4, 128),
        ),
        (
            got3, norm_one, norm_two, hidden_two, slope_two, second, feat, up_hbm, near_rows, far_rows,
            gain3, bias3, expand, real,
        ),
        [pltpu.VMEM((pairs * sizes.ext, 2 * wide), BF16)],
    )
    got4 = exchange(rows, count)
    gradgain3, gradbias3, gradgain2, gradbias2, grad_one, activated, rows = call(
        backward_kernel,
        (
            shape(1, 256),
            shape(1, 256),
            shape(1, 64),
            shape(1, 64),
            shape(pairs, own, 128),
            shape(*flat, dtype=BF16),
            shape(count * sizes.rows5, 128, dtype=BF16),
        ),
        (
            got4, got3, norm_one, norm_two, norm_three, gram, windows, slope_one, first, hidden_two,
            slope_two, second, back, raw, feat, sums, gain2, expand, conv_back, active, image_counts,
        ),
        [pltpu.VMEM((sizes.wide2, 128), F32)] * 2
        + masks
        + [
            pltpu.VMEM((pairs * own, 384), BF16),
            pltpu.VMEM((count * sizes.rows5, 128), F32),
            pltpu.SemaphoreType.DMA,
        ],
        away=(5,),
    )
    got5 = exchange(rows, count)
    gradgain1, gradbias1, feature_grad, rows = call(
        shares_kernel,
        (
            shape(1, 64),
            shape(1, 64),
            pltpu.VMEM(deep, BF16),
            shape(count * sizes.rows6, 128, dtype=BF16),
        ),
        (got5, got1, got2, got3, norm_one, gain1, grad_one, first, grad_sum, weight, real),
        [pltpu.VMEM((count * sizes.rows6, 128), F32), pltpu.VMEM((count * sizes.rows5, 128), F32)],
    )
    got6 = exchange(rows, count)
    redt_grad, expander_grad, spatial_grad = call(
        weights_kernel,
        (shape(64, 256), shape(64, 256), shape(9 * 64, 64)),
        (got6,),
        [pltpu.VMEM((count * sizes.rows6, 128), F32)],
    )
    return (
        activated.reshape(features.shape),
        feature_grad.reshape(features.shape),
        redt_grad.T,
        spatial_grad.reshape(spatial.shape),
        expander_grad,
        gradgain1.reshape(64),
        gradbias1.reshape(64),
        gradgain2.reshape(64),
        gradbias2.reshape(64),
        gradgain3.reshape(256),
        gradbias3.reshape(256),
    )


def solution(mesh):
    whole = P("img", "ha", None, None)
    in_specs = (whole,) + (P(),) * 9 + (whole, P("img"))
    out_specs = (whole, whole) + (P(),) * 9
    return jax.shard_map(
        on_device, mesh=mesh, in_specs=in_specs, out_specs=out_specs, check_vma=False
    )
```

time: 588 us -> 83.3 us (0.14)
  blocking collectives: 365 us -> 54.9 us
  waiting for transfers between devices: 127 us -> 7.26 us
  matrix products: 32.6 us -> 0 us
  other arithmetic: 31.3 us -> 0 us
  Pallas kernels: 0 us -> 14.5 us
  between operations: 15.2 us -> 1.41 us
    psum x9 -> x0, blocking collectives: 365 us -> none  [the longest x3 123 us: moments(): lax.psum((jnp.sum(values * pixmask, axis=(0, 1, 2)), local_total), ('img'...]
    psum x1 -> x0, waiting for transfers between devices: 124 us -> none  [on_device(): reducer_grad = lax.psum(reducer_local, ('img', 'ha'))]
    all_to_all x0 -> x5, blocking collectives: none -> 54.9 us  [exchange(): return lax.all_to_all(parted, AXES, 0, 0).reshape(rows.shape)]
    dot_general x33 -> x0, matrix products: 32.6 us -> none  [the longest x9 7.29 us: on_device(): jnp.einsum('irwc,cd->irwd', window, spatial[vertical, lateral], preferred...]
    pallas_call x0 -> x8, Pallas kernels: none -> 14.5 us  [call(): pl.pallas_call(functools.partial(kernel, sizes), out_shape=outs, in_specs...]
    reduce_sum x4 -> x0, other arithmetic: 12.3 us -> none  [the longest x1 6.22 us: norm_back(): jnp.sum(grad_pre, axis=(0, 1, 2))]
    convert_element_type x5 -> x0, other arithmetic: 10.6 us -> none  [the longest x1 4.49 us: on_device(): grad_third = grad_third.astype(jnp.bfloat16)]
    all_to_all x0 -> x1, waiting for transfers between devices: none -> 7.26 us  [exchange(): return lax.all_to_all(parted, AXES, 0, 0).reshape(rows.shape)]
  transfers between devices with their start and end apart: 5 -> 3, of which waited for: 2 -> 1; matrix products, arithmetic and copies ran while one was open for 1% -> 1% of each run, Pallas kernels for 0% -> 1%
where the time goes in v1:
time: 83.3 us; the launch traced here: 83 us
  blocking collectives  54.9 us (66%)
  Pallas kernels  14.5 us (17%)
  waiting for transfers between devices  7.26 us (9%)
  starting transfers between devices  3.77 us (5%)
  between operations  1.41 us (2%)
  local copies, waits for them, and re-layouts  1.2 us (1%)
    all_to_all x5, blocking collectives, exchange(): return lax.all_to_all(parted, AXES, 0, 0).reshape(rows.shape)  54.9 us
    pallas_call x8, Pallas kernels, call(): pl.pallas_call(functools.partial(kernel, sizes), out_shape=outs, in_specs...  14.5 us
    all_to_all x1, waiting for transfers between devices, exchange(): return lax.all_to_all(parted, AXES, 0, 0).reshape(rows.shape)  7.26 us
    all_to_all x1, starting transfers between devices, exchange(): return lax.all_to_all(parted, AXES, 0, 0).reshape(rows.shape)  2.58 us
  transfers between devices with their start and end apart: 3, of which 1 were waited for; matrix products, arithmetic and copies ran while one was open for 1% of the time, Pallas kernels for 1%

profile of v1, /device:TPU:0, one launch (start us, length us, event | category | flops | bytes accessed | tf_op | source)
XLA Modules:
  0.0 83.0 jit_solution(12725389917018181553)
XLA Ops:
  1.3 0.0 copy-start
  1.3 1.5 %shard_map.203 = (bf16[128,512]{1,0:T(8,128)(2,1)S(1)}, bf16[2,256,256]{2,1,0:T(8,128)(2,1)S(1)}, bf16[2,256,256]{2,1,0:T(8,128)(2,1)S(1)}, bf16[128,512]{1,0:T(...) custom-call(bf16[2,2,784,256]{3,2,1,0:T(8,128)(2,1)} %bitcast.37, ...), custom_call_target="tpu_custom_call" | custom-call | tf_op jit(solution)/shard_map/pallas_call | solution.py:858
  2.8 0.0 copy-start.3
  2.8 0.0 copy-start.6
  2.9 0.5 collective-permute-start
  3.4 0.7 collective-permute-start.1
  4.1 0.0 copy-done
  4.1 0.8 shard_map.204
  4.9 15.9 %all_to_all.30 = f32[32,4,1,128]{3,1,2,0:T(4,128)S(1)} all-to-all(f32[32,4,1,128]{3,1,2,0:T(4,128)S(1)} %bitcast.59), channel_id=1, replica_groups=mesh['img'=8,'ha'=4] {'img','ha'}, dimensions={0} | all-to-all | bytes 131072 | tf_op jit(solution)/shard_map/all_to_all | solution.py:817
  20.8 0.0 collective-permute-done.near_ref
  20.8 0.0 collective-permute-done.1.far_ref
  20.8 0.0 copy-done.3
  20.8 0.0 copy-done.6
  20.8 0.0 copy-start.2
  20.8 0.0 copy-start.7
  20.9 1.9 %shard_map.205 = (bf16[2,784,384]{2,1,0:T(8,128)(2,1)S(1)}, f32[2,784,128]{2,1,0:T(8,128)S(1)}, f32[2,896,128]{2,1,0:T(8,128)S(1)}, f32[8,128]{1,0:T(8,128)S(1)}...) custom-call(f32[128,128]{1,0:T(8,128)S(1)} %bitcast.47, bf16[2,2,784,256]{3,2,1,0:T(8,128)(2,1)S(1)} %bitcast.39, ...), custom_call_target="tpu_custom_call" | custom-call | tf_op jit(solution)/shard_map/pallas_call | solution.py:858
  22.8 9.2 %all_to_all.31 = f32[32,4,1,128]{3,1,2,0:T(4,128)S(1)} all-to-all(f32[32,4,1,128]{3,1,2,0:T(4,128)S(1)} %bitcast.58), channel_id=1, replica_groups=mesh['img'=8,'ha'=4] {'img','ha'}, dimensions={0} | all-to-all | bytes 131072 | tf_op jit(solution)/shard_map/all_to_all | solution.py:817
  32.0 0.0 copy-done.2
  32.0 0.0 copy-done.7
  32.0 1.5 %shard_map.206 = (bf16[2,896,128]{2,1,0:T(8,128)(2,1)S(1)}, f32[2,896,128]{2,1,0:T(8,128)S(1)}, f32[8,128]{1,0:T(8,128)S(1)}, f32[64,128]{1,0:T(8,128)S(1)}, f32[224,128]{1,0:T(8,128)S(1)}) custom-call(f32[128,128]{1,0:T(8,128)S(1)} %bitcast.51, f32[128,128]{1,0:T(8,128)S(1)} %bitcast.48, f32[2,896,128]{2,1,0:T(8,128)S(1)} %get-tuple-element.60.second_ref, ...), custom_call_target="tpu_custom_call" | custom-call | tf_op jit(solution)/shard_map/pallas_call | solution.py:858
  33.6 9.7 %all_to_all.32 = f32[32,7,1,128]{3,2,1,0:T(1,128)S(1)} all-to-all(f32[32,7,1,128]{3,2,1,0:T(1,128)S(1)} %bitcast.57), channel_id=1, replica_groups=mesh['img'=8,'ha'=4] {'img','ha'}, dimensions={0} | all-to-all | bytes 229376 | tf_op jit(solution)/shard_map/all_to_all | solution.py:817
  43.3 0.0 copy-done.1
  43.3 0.0 copy-done.4
  43.3 3.0 %shard_map.207 = (bf16[3136,256]{1,0:T(8,128)(2,1)S(1)}, f32[3136,256]{1,0:T(8,128)S(1)}, f32[2,896,128]{2,1,0:T(8,128)S(1)}, f32[8,256]{1,0:T(8,128)S(1)}, f32[...) custom-call(f32[224,128]{1,0:T(8,128)S(1)} %bitcast.44, f32[8,128]{1,0:T(8,128)S(1)} %get-tuple-element.64.norm_one_ref, ...), custom_call_target="tpu_custom_call" | custom-call | tf_op jit(solution)/shard_map/pallas_call | solution.py:858
  46.3 9.7 %all_to_all.33 = f32[32,7,1,128]{3,2,1,0:T(1,128)S(1)} all-to-all(f32[32,7,1,128]{3,2,1,0:T(1,128)S(1)} %bitcast.56), channel_id=1, replica_groups=mesh['img'=8,'ha'=4] {'img','ha'}, dimensions={0} | all-to-all | bytes 229376 | tf_op jit(solution)/shard_map/all_to_all | solution.py:817
  56.0 3.8 %shard_map.208 = (f32[1,256]{1,0:T(1,128)}, f32[1,256]{1,0:T(1,128)}, f32[1,64]{1,0:T(1,128)}, f32[1,64]{1,0:T(1,128)}, f32[2,784,128]{2,1,0:T(8,128)S(1)}, /*in...) custom-call(f32[224,128]{1,0:T(8,128)S(1)} %bitcast.54, f32[224,128]{1,0:T(8,128)S(1)} %bitcast.45, ...), custom_call_target="tpu_custom_call" | custom-call | tf_op jit(solution)/shard_map/pallas_call | solution.py:858
  59.8 10.3 %all_to_all.34 = bf16[32,10,2,128]{3,2,1,0:T(2,128)(2,1)S(1)} all-to-all(bf16[32,10,2,128]{3,2,1,0:T(2,128)(2,1)S(1)} %bitcast.55), channel_id=1, replica_groups=mesh['img'=8,'ha'=4] {'img','ha'}, dimensions={0} | all-to-all | bytes 327680 | tf_op jit(solution)/shard_map/all_to_all | solution.py:817
  70.1 1.0 %shard_map.209 = (f32[1,64]{1,0:T(1,128)}, f32[1,64]{1,0:T(1,128)}, bf16[2,2,784,256]{3,2,1,0:T(8,128)(2,1)S(1)}, bf16[576,128]{1,0:T(8,128)(2,1)}) custom-call(bf16[640,128]{1,0:T(8,128)(2,1)S(1)} %bitcast.50, f32[128,128]{1,0:T(8,128)S(1)} %bitcast.49, f32[128,128]{1,0:T(8,128)S(1)} %bitcast.52, f32[224,128]{1,0:T(8,128)S(1)} %bitcast.46, ...), custom_call_target="tpu_custom_call" | custom-call | tf_op jit(solution)/shard_map/pallas_call | solution.py:858
  71.1 2.6 %all-to-all-start.5 = ((bf16[32,9,2,128]{3,2,1,0:T(2,128)(2,1)}), bf16[32,9,2,128]{3,2,1,0:T(2,128)(2,1)S(1)}, u32[]{:S(2)}, u32[]{:S(2)}) async-start(bf16[32,9,2,128]{3,2,1,0:T(2,128)(2,1)} %bitcast.24), calls=%async_computation.5 | async-start | bytes 294912 | tf_op jit(solution)/shard_map/all_to_all | solution.py:817
  73.7 1.2 %copy.27 = bf16[4,14,56,256]{3,2,1,0:T(8,128)(2,1)} copy(bf16[4,14,56,256]{3,2,1,0:T(8,128)(2,1)S(1)} %bitcast.36) | data formatting | bytes 3211264
  74.9 7.3 %all-to-all-done.5 = bf16[32,9,2,128]{3,2,1,0:T(2,128)(2,1)S(1)} async-done(((bf16[32,9,2,128]{3,2,1,0:T(2,128)(2,1)}), bf16[32,9,2,128]{3,2,1,0:T(2,128)(2,1)S(1)}, u32[]{:S(2)}, u32[]{:S(2)}) %all-to-all-start.5) | async-done | bytes 147488 | tf_op jit(solution)/shard_map/all_to_all | solution.py:817
  82.1 0.8 shard_map.210
  (4 shorter events, 0.0 us)
Async XLA Ops:
  1.3 2.8 %copy-start = (bf16[4,14,56,256]{3,2,1,0:T(8,128)(2,1)S(1)}, bf16[4,14,56,256]{3,2,1,0:T(8,128)(2,1)}, u32[]{:S(2)}) copy-start(bf16[4,14,56,256]{3,2,1,0:T(8,128)(2,1)} %param.12) | copy-start | bytes 4816900
  2.8 18.0 %copy-start.3 = (f32[64]{0:T(128)S(1)}, f32[64]{0:T(128)}, u32[]{:S(2)}) copy-start(f32[64]{0:T(128)} %param.16) | copy-start | bytes 772
  2.8 18.0 %copy-start.6 = (f32[64]{0:T(128)S(1)}, f32[64]{0:T(128)}, u32[]{:S(2)}) copy-start(f32[64]{0:T(128)} %param.17) | copy-start | bytes 772
  2.9 18.0 %collective-permute-start = (bf16[2,2,2,112,256]{4,3,2,1,0:T(8,128)(2,1)S(1)}, bf16[2,2,2,112,256]{4,3,2,1,0:T(8,128)(2,1)S(1)}, u32[]{:S(2)}, u32[]{:S(2)}) collective-permute-start(bf16[2,2,2,112,256]{4,3,2,1,0:T(8,128)(2,1)S(1)} %get-tuple-element.56), channel_id=1, source_target_pairs={{0,1},{1,0},{2,3},{3,2},{4,5},{5,4},{6,7},{7,6},{8,9},{9,8},{10,11... | collective-permute-start | bytes 1376264 | tf_op jit(solution)/shard_map/ppermute | solution.py:898
  3.4 17.4 %collective-permute-start.1 = (bf16[2,2,2,112,256]{4,3,2,1,0:T(8,128)(2,1)S(1)}, bf16[2,2,2,112,256]{4,3,2,1,0:T(8,128)(2,1)S(1)}, u32[]{:S(2)}, u32[]{:S(2)}) collective-permute-start(bf16[2,2,2,112,256]{4,3,2,1,0:T(8,128)(2,1)S(1)} %get-tuple-element.57), channel_id=1, source_target_pairs={{1,2},{2,1},{5,6},{6,5},{9,10},{10,9},{13,14},{14,13},{17,18},{18,... | collective-permute-start | bytes 1376264 | tf_op jit(solution)/shard_map/ppermute | solution.py:899
  20.8 11.2 %copy-start.2 = (f32[64]{0:T(128)S(1)}, f32[64]{0:T(128)}, u32[]{:S(2)}) copy-start(f32[64]{0:T(128)} %param.18) | copy-start | bytes 772
  20.8 11.2 %copy-start.7 = (f32[64]{0:T(128)S(1)}, f32[64]{0:T(128)}, u32[]{:S(2)}) copy-start(f32[64]{0:T(128)} %param.19) | copy-start | bytes 772
  22.8 20.5 %copy-start.1 = (bf16[4,14,56,256]{3,2,1,0:T(8,128)(2,1)S(1)}, bf16[4,14,56,256]{3,2,1,0:T(8,128)(2,1)}, u32[]{:S(2)}) copy-start(bf16[4,14,56,256]{3,2,1,0:T(8,128)(2,1)} %param.22) | copy-start | bytes 4816900
  22.8 20.5 %copy-start.4 = (f32[256]{0:T(256)S(1)}, f32[256]{0:T(256)}, u32[]{:S(2)}) copy-start(f32[256]{0:T(256)} %param.20) | copy-start | bytes 3076
  22.8 20.5 %copy-start.5 = (f32[256]{0:T(256)S(1)}, f32[256]{0:T(256)}, u32[]{:S(2)}) copy-start(f32[256]{0:T(256)} %param.21) | copy-start | bytes 3076
  71.1 11.0 %all-to-all-start.5 = ((bf16[32,9,2,128]{3,2,1,0:T(2,128)(2,1)}), bf16[32,9,2,128]{3,2,1,0:T(2,128)(2,1)S(1)}, u32[]{:S(2)}, u32[]{:S(2)}) async-start(bf16[32,9,2,128]{3,2,1,0:T(2,128)(2,1)} %bitcast.24), calls=%async_computation.5 | async-start | bytes 294912 | tf_op jit(solution)/shard_map/all_to_all | solution.py:817

commit v2 on v1

--- a/solution.py
+++ b/solution.py
@@ -192,6 +192,17 @@
     high_ref[...] = (column < sizes.across - 1).astype(F32)
 
 
+def all_taps(out_ref, taps_ref, back):
+    out_ref[...] = jnp.zeros(out_ref.shape, BF16)
+    for vertical in range(3):
+        for lateral in range(3):
+            tap = taps_ref[(vertical * 3 + lateral) * 64 : (vertical * 3 + lateral + 1) * 64, :]
+            if back:
+                place_taps(out_ref, 2 - vertical, lateral, jnp.transpose(tap))
+            else:
+                place_taps(out_ref, vertical, lateral, tap)
+
+
 def place_taps(out_ref, vertical, lateral, tap):
     for half in range(2):
         row = vertical * 64 if vertical < 2 else 128 + 64 * half
@@ -249,17 +260,9 @@
 
 
 def prepare_kernel(
-    sizes, feat_hbm, up_hbm, redt_hbm, taps_hbm, expander_hbm, count_ref,
-    weight_ref, conv_ref, back_ref, expand_ref, real_ref, near_ref, far_ref,
-    redt_ref, taps_ref, expander_ref, edge_sem, small_sem,
+    sizes, feat_hbm, up_hbm, redt_hbm, count_ref, weight_ref, real_ref, near_ref, far_ref, redt_ref, sem_ref,
 ):
     step, own = sizes.step, sizes.own
-    small = [
-        pltpu.make_async_copy(source, target, small_sem.at[index])
-        for index, (source, target) in enumerate(
-            ((redt_hbm, redt_ref), (expander_hbm, expander_ref), (taps_hbm, taps_ref))
-        )
-    ]
     edges = []
     odd = lax.rem(lax.axis_index("ha"), 2)
     to_last = pl.multiple_of((1 - odd) * (own - step), step)
@@ -267,25 +270,15 @@
     for out, start in ((near_ref, to_last), (far_ref, to_head)):
         for place, source in enumerate((feat_hbm, up_hbm)):
             copy = pltpu.make_async_copy(
-                source.at[:, :, pl.ds(start, step), :], out.at[place], edge_sem.at[len(edges)]
+                source.at[:, :, pl.ds(start, step), :], out.at[place], sem_ref.at[len(edges)]
             )
             copy.start()
             edges.append(copy)
-    for copy in small:
-        copy.start()
-    conv_ref[...] = jnp.zeros(conv_ref.shape, BF16)
-    back_ref[...] = jnp.zeros(back_ref.shape, BF16)
-    for copy in small:
-        copy.wait()
+    small = pltpu.make_async_copy(redt_hbm, redt_ref, sem_ref.at[4])
+    small.start()
     fill_real(sizes, real_ref, count_ref[0])
+    small.wait()
     diagonal(weight_ref, redt_ref[...])
-    diagonal(expand_ref, expander_ref[...])
-    for vertical in range(3):
-        for lateral in range(3):
-            tap = taps_ref[(vertical * 3 + lateral) * 64 : (vertical * 3 + lateral + 1) * 64, :]
-            turned = jnp.transpose(tap)
-            place_taps(conv_ref, vertical, lateral, tap)
-            place_taps(back_ref, 2 - vertical, lateral, turned)
     for copy in edges:
         copy.wait()
 
@@ -329,8 +322,8 @@
 
 
 def conv_kernel(
-    sizes, got_ref, feat_ref, first_ref, near_ref, far_ref, weight_ref, conv_ref, gain_ref, bias_ref, real_ref,
-    window_ref, slope_ref, second_ref, norm_ref, cross_ref, out_ref, hidden_ref, turned_ref, low_ref, high_ref, normed_ref,
+    sizes, got_ref, feat_ref, first_ref, near_ref, far_ref, weight_ref, taps_ref, gain_ref, bias_ref, real_ref,
+    window_ref, slope_ref, second_ref, norm_ref, cross_ref, out_ref, conv_ref, hidden_ref, turned_ref, low_ref, high_ref, normed_ref,
 ):
     pairs, step, own, across = sizes.pairs, sizes.step, sizes.own, sizes.across
     numbers = got_ref[pl.ds(1, sizes.count, stride=sizes.rows1), :]
@@ -343,6 +336,7 @@
     near_start = pl.multiple_of((1 - odd) * (own + step), step)
     far_start = pl.multiple_of(odd * (own + step), step)
     edge_masks(sizes, low_ref, high_ref)
+    all_taps(conv_ref, taps_ref, False)
     for g in range(pairs):
         mask = pair_mask(real_ref, g)
 
@@ -427,8 +421,8 @@
 
 
 def middle_kernel(
-    sizes, got_ref, first_got_ref, second_ref, gain_ref, bias_ref, expand_ref, cross_ref, real_ref,
-    hidden_ref, slope_ref, norm_ref, gram_ref, out_ref, left_ref, right_ref,
+    sizes, got_ref, first_got_ref, second_ref, gain_ref, bias_ref, expander_ref, cross_ref, real_ref,
+    hidden_ref, slope_ref, norm_ref, gram_ref, expand_ref, out_ref, left_ref, right_ref,
 ):
     pairs, step, own = sizes.pairs, sizes.step, sizes.own
     slots = sizes.rows3
@@ -436,6 +430,7 @@
     average, inverse, _ = merged(sizes, got_ref, sizes.rows2, numbers)
     gain, bias = twice(gain_ref[...]), twice(bias_ref[...])
     centre, tangent = swish(bias)
+    diagonal(expand_ref, expander_ref[...])
     sums = (jnp.zeros((8, 128), F32),) * 3
     for g in range(pairs):
         mask = pair_mask(real_ref, g)
@@ -472,7 +467,7 @@
     slopes = slopes + columns(apart)[0:64, :] * tangent
     gram = jnp.where(wide, gram, 0.0)
     gram_ref[...] = gram
-    weights = expand_ref[0:64, 0:256]
+    weights = expander_ref[...]
     quad = total_of(exact(nn, gram[:, 0:64], weights) * weights.astype(F32))
     norm_ref[...] = jnp.concatenate(
         [average, inverse, centre, apart, jnp.where(low_lanes((1, 128)), slope, tilted), jnp.zeros((3, 128), F32)],
@@ -521,7 +516,7 @@
     flat = scale * middle
     (flat_back,) = exact_rows(nt, [flat], expand_ref[:, 0:256] + expand_ref[:, 256:512])
     last_ref[...] = jnp.concatenate(
-        [average, inverse, scale, jnp.concatenate([mean_hidden, apart], axis=1), middle, flat, jnp.zeros((2, 256), F32)],
+        [average, inverse, scale, jnp.concatenate([mean_hidden, apart], axis=1), middle, flat, shift, jnp.zeros((1, 256), F32)],
         axis=0,
     )
     biases = jnp.zeros((8, 256), F32)
@@ -596,9 +591,9 @@
 def backward_kernel(
     sizes, got_ref, third_got_ref, norm_one_ref, norm_ref, last_ref, gram_ref, window_ref, slope_one_ref,
     first_ref, hidden_ref, slope_ref, second_ref, back_ref, raw_ref, feat_ref, sums_ref, gain_two_ref, expand_ref,
-    conv_back_ref, active_ref, count_ref,
+    taps_ref, active_ref, count_ref,
     gain3_out_ref, bias3_out_ref, gain2_out_ref, bias2_out_ref, grad_one_ref, active_hbm, out_ref,
-    grad_ref, turned_ref, low_ref, high_ref, right_ref, send_ref, sem_ref,
+    conv_back_ref, grad_ref, turned_ref, low_ref, high_ref, right_ref, send_ref, sem_ref,
 ):
     pairs, step, own, across = sizes.pairs, sizes.step, sizes.own, sizes.across
     leave = pltpu.make_async_copy(active_ref, active_hbm, sem_ref)
@@ -618,14 +613,13 @@
     diag = expand_ref[...]
     stacked = diag[:, 0:256] + diag[:, 256:512]
     flat_here = flat - last_ref[5:6, :]
-    flat_back, flat_here_back = exact_rows(nt, [flat, flat_here], stacked)
+    flat_back, flat_here_back, mean_mix, apart_mix = exact_rows(
+        nt, [flat, flat_here, last_ref[0:1, :] * tilt, last_ref[6:7, :] * tilt], stacked
+    )
     tilt_wide = jnp.concatenate([tilt, tilt], axis=1)
     mixing = exact(nt, diag.astype(F32) * tilt_wide, diag)
     mix_high, mix_low, _ = pieces(mixing)
     mix_both = jnp.concatenate([mix_high, mix_low], axis=1)
-    mean_mix, apart_mix = [
-        row[:, 0:128] + row[:, 128:256] for row in exact_rows(nn, [mean_hidden, apart], mix_both)
-    ]
     row_low = low_lanes((1, 128))
     slopes = get_sum(third_got_ref, 3, third_slots, count)
     cross = get_rows(got_ref, 5, slots, count, 64)
@@ -641,6 +635,7 @@
     has_above = (place > 0).astype(F32)
     has_below = (place < lax.axis_size("ha") - 1).astype(F32)
     edge_masks(sizes, low_ref, high_ref)
+    all_taps(conv_back_ref, taps_ref, True)
     average_one, inverse_one = norm_one_ref[0:1, :], norm_one_ref[1:2, :]
 
     local = norm_ref[3:4, :]
@@ -838,6 +833,7 @@
     flat = (images * own, wide)
     deep = (2, pairs, own, wide)
     feat_hbm, up_hbm = features.reshape(deep), upstream.reshape(deep)
+    taps = spatial.reshape(9 * 64, 64)
     gain1, bias1, gain2, bias2, gain3, bias3 = [
         value.reshape(1, value.shape[0])
         for value in (gain_reduce, bias_reduce, gain_spatial, bias_spatial, gain_expand, bias_expand)
@@ -872,27 +868,18 @@
 
     given = tuple(
         pltpu.with_memory_space_constraint(value, pltpu.HBM)
-        for value in (feat_hbm, up_hbm, reducer.T, spatial.reshape(9 * 64, 64), expander)
-    )
-    weight, conv, conv_back, expand, real, near_rows, far_rows = call(
+        for value in (feat_hbm, up_hbm, reducer.T)
+    )
+    weight, real, near_rows, far_rows = call(
         prepare_kernel,
         (
-            shape(128, 512, dtype=BF16),
-            shape(2, 256, 256, dtype=BF16),
-            shape(2, 256, 256, dtype=BF16),
             shape(128, 512, dtype=BF16),
             shape(16, 256),
             shape(2, 2, pairs, step, wide, dtype=BF16),
             shape(2, 2, pairs, step, wide, dtype=BF16),
         ),
         (*given, image_counts),
-        [
-            pltpu.VMEM((64, 256), BF16),
-            pltpu.VMEM((9 * 64, 64), BF16),
-            pltpu.VMEM((64, 256), BF16),
-            pltpu.SemaphoreType.DMA((4,)),
-            pltpu.SemaphoreType.DMA((3,)),
-        ],
+        [pltpu.VMEM((64, 256), BF16), pltpu.SemaphoreType.DMA((5,))],
         far=given,
     )
     near_rows = lax.ppermute(near_rows, "ha", near)
@@ -914,20 +901,21 @@
             shape(64, 256),
             shape(count * sizes.rows2, 128),
         ),
-        (got1, feat, first, near_rows, far_rows, weight, conv, gain1, bias1, real),
-        [pltpu.VMEM((pairs, sizes.wide1, 128), F32)] * 2 + [*masks, pltpu.VMEM((pairs * own, 128), BF16)],
+        (got1, feat, first, near_rows, far_rows, weight, taps, gain1, bias1, real),
+        [pltpu.VMEM((2, 256, 256), BF16)] + [pltpu.VMEM((pairs, sizes.wide1, 128), F32)] * 2 + [*masks, pltpu.VMEM((pairs * own, 128), BF16)],
     )
     got2 = exchange(rows, count)
-    hidden_two, slope_two, norm_two, gram, rows = call(
+    hidden_two, slope_two, norm_two, gram, expand, rows = call(
         middle_kernel,
         (
             shape(pairs, sizes.ext, 128, dtype=BF16),
             shape(pairs, sizes.ext, 128),
             shape(8, 128),
             shape(64, 128),
+            shape(128, 512, dtype=BF16),
             shape(count * sizes.rows3, 128),
         ),
-        (got2, got1, second, gain2, bias2, expand, cross, real),
+        (got2, got1, second, gain2, bias2, expander, cross, real),
         [pltpu.VMEM((pairs * own, 128), BF16), pltpu.VMEM((pairs * own, 384), BF16)],
     )
     got3 = exchange(rows, count)
@@ -961,9 +949,10 @@
         ),
         (
             got4, got3, norm_one, norm_two, norm_three, gram, windows, slope_one, first, hidden_two,
-            slope_two, second, back, raw, feat, sums, gain2, expand, conv_back, active, image_counts,
+            slope_two, second, back, raw, feat, sums, gain2, expand, taps, active, image_counts,
         ),
-        [pltpu.VMEM((sizes.wide2, 128), F32)] * 2
+        [pltpu.VMEM((2, 256, 256), BF16)]
+        + [pltpu.VMEM((sizes.wide2, 128), F32)] * 2
         + masks
         + [
             pltpu.VMEM((pairs * own, 384), BF16),

time: 83.3 us -> 83 us (level)
  no operation moved by 1% of the time
where the time goes in v2:
time: 83 us; the launch traced here: 82.7 us
  blocking collectives  54.7 us (66%)
  Pallas kernels  14.2 us (17%)
  waiting for transfers between devices  7.26 us (9%)
  starting transfers between devices  3.77 us (5%)
  between operations  1.46 us (2%)
  local copies, waits for them, and re-layouts  1.22 us (1%)
    all_to_all x5, blocking collectives, exchange(): return lax.all_to_all(parted, AXES, 0, 0).reshape(rows.shape)  54.7 us
    pallas_call x8, Pallas kernels, call(): pl.pallas_call(functools.partial(kernel, sizes), out_shape=outs, in_specs...  14.2 us
    all_to_all x1, waiting for transfers between devices, exchange(): return lax.all_to_all(parted, AXES, 0, 0).reshape(rows.shape)  7.26 us
    all_to_all x1, starting transfers between devices, exchange(): return lax.all_to_all(parted, AXES, 0, 0).reshape(rows.shape)  2.58 us
  transfers between devices with their start and end apart: 3, of which 1 were waited for; matrix products, arithmetic and copies ran while one was open for 1% of the time, Pallas kernels for 1%

profile of v2, /device:TPU:0, one launch (start us, length us, event | category | flops | bytes accessed | tf_op | source)
XLA Modules:
  0.0 82.7 jit_solution(9094591827109654484)
XLA Ops:
  1.3 0.0 copy-start
  1.3 1.4 %shard_map.203 = (bf16[128,512]{1,0:T(8,128)(2,1)S(1)}, f32[16,256]{1,0:T(8,128)S(1)}, bf16[2,2,2,112,256]{4,3,2,1,0:T(8,128)(2,1)S(1)}, bf16[2,2,2,112,256]{4,3,2,1,0:T(8,128)(2,1)S(1)}) custom-call(bf16[2,2,784,256]{3,2,1,0:T(8,128)(2,1)} %bitcast.37, bf16[2,2,784,256]{3,2,1,0:T(8,128)(2,1)} %bitcast.42, bf16[64,256]{1,0:T(8,128)(2,1)} %bitcast.70, ...), custom_call_target="tpu_custom_call" | custom-call | tf_op jit(solution)/shard_map/pallas_call | solution.py:854
  2.7 0.0 copy-start.2
  2.8 0.0 copy-start.5
  2.8 0.0 copy-start.8
  2.8 0.5 collective-permute-start
  3.3 0.7 collective-permute-start.1
  4.0 0.8 shard_map.204
  4.8 15.9 %all_to_all.30 = f32[32,4,1,128]{3,1,2,0:T(4,128)S(1)} all-to-all(f32[32,4,1,128]{3,1,2,0:T(4,128)S(1)} %bitcast.61), channel_id=1, replica_groups=mesh['img'=8,'ha'=4] {'img','ha'}, dimensions={0} | all-to-all | bytes 131072 | tf_op jit(solution)/shard_map/all_to_all | solution.py:812
  20.7 0.0 collective-permute-done.near_ref
  20.7 0.0 collective-permute-done.1.far_ref
  20.7 0.0 copy-done.5
  20.7 0.0 copy-done.8
  20.7 0.0 copy-start.3
  20.7 0.0 copy-start.4
  20.8 0.0 copy-start.9
  20.8 0.0 copy-start.1
  20.8 0.0 copy-start.6
  20.8 0.0 copy-start.7
  20.8 1.9 %shard_map.205 = (bf16[2,784,384]{2,1,0:T(8,128)(2,1)S(1)}, f32[2,784,128]{2,1,0:T(8,128)S(1)}, f32[2,896,128]{2,1,0:T(8,128)S(1)}, f32[8,128]{1,0:T(8,128)S(1)}...) custom-call(f32[128,128]{1,0:T(8,128)S(1)} %bitcast.47, bf16[2,2,784,256]{3,2,1,0:T(8,128)(2,1)S(1)} %bitcast.39, ...), custom_call_target="tpu_custom_call" | custom-call | tf_op jit(solution)/shard_map/pallas_call | solution.py:854
  22.7 9.1 %all_to_all.31 = f32[32,4,1,128]{3,1,2,0:T(4,128)S(1)} all-to-all(f32[32,4,1,128]{3,1,2,0:T(4,128)S(1)} %bitcast.60), channel_id=1, replica_groups=mesh['img'=8,'ha'=4] {'img','ha'}, dimensions={0} | all-to-all | bytes 131072 | tf_op jit(solution)/shard_map/all_to_all | solution.py:812
  31.8 1.5 %shard_map.206 = (bf16[2,896,128]{2,1,0:T(8,128)(2,1)S(1)}, f32[2,896,128]{2,1,0:T(8,128)S(1)}, f32[8,128]{1,0:T(8,128)S(1)}, f32[64,128]{1,0:T(8,128)S(1)}, bf1...) custom-call(f32[128,128]{1,0:T(8,128)S(1)} %bitcast.51, f32[128,128]{1,0:T(8,128)S(1)} %bitcast.48, ...), custom_call_target="tpu_custom_call" | custom-call | tf_op jit(solution)/shard_map/pallas_call | solution.py:854
  33.3 9.7 %all_to_all.32 = f32[32,7,1,128]{3,2,1,0:T(1,128)S(1)} all-to-all(f32[32,7,1,128]{3,2,1,0:T(1,128)S(1)} %bitcast.59), channel_id=1, replica_groups=mesh['img'=8,'ha'=4] {'img','ha'}, dimensions={0} | all-to-all | bytes 229376 | tf_op jit(solution)/shard_map/all_to_all | solution.py:812
  43.1 3.0 %shard_map.207 = (bf16[3136,256]{1,0:T(8,128)(2,1)S(1)}, f32[3136,256]{1,0:T(8,128)S(1)}, f32[2,896,128]{2,1,0:T(8,128)S(1)}, f32[8,256]{1,0:T(8,128)S(1)}, f32[...) custom-call(f32[224,128]{1,0:T(8,128)S(1)} %bitcast.44, f32[8,128]{1,0:T(8,128)S(1)} %get-tuple-element.60.norm_one_ref, ...), custom_call_target="tpu_custom_call" | custom-call | tf_op jit(solution)/shard_map/pallas_call | solution.py:854
  46.1 9.7 %all_to_all.33 = f32[32,7,1,128]{3,2,1,0:T(1,128)S(1)} all-to-all(f32[32,7,1,128]{3,2,1,0:T(1,128)S(1)} %bitcast.58), channel_id=1, replica_groups=mesh['img'=8,'ha'=4] {'img','ha'}, dimensions={0} | all-to-all | bytes 229376 | tf_op jit(solution)/shard_map/all_to_all | solution.py:812
  55.8 3.7 %shard_map.208 = (f32[1,256]{1,0:T(1,128)}, f32[1,256]{1,0:T(1,128)}, f32[1,64]{1,0:T(1,128)}, f32[1,64]{1,0:T(1,128)}, f32[2,784,128]{2,1,0:T(8,128)S(1)}, /*in...) custom-call(f32[224,128]{1,0:T(8,128)S(1)} %bitcast.56, f32[224,128]{1,0:T(8,128)S(1)} %bitcast.45, ...), custom_call_target="tpu_custom_call" | custom-call | tf_op jit(solution)/shard_map/pallas_call | solution.py:854
  59.5 10.3 %all_to_all.34 = bf16[32,10,2,128]{3,2,1,0:T(2,128)(2,1)S(1)} all-to-all(bf16[32,10,2,128]{3,2,1,0:T(2,128)(2,1)S(1)} %bitcast.57), channel_id=1, replica_groups=mesh['img'=8,'ha'=4] {'img','ha'}, dimensions={0} | all-to-all | bytes 327680 | tf_op jit(solution)/shard_map/all_to_all | solution.py:812
  69.8 1.0 %shard_map.209 = (f32[1,64]{1,0:T(1,128)}, f32[1,64]{1,0:T(1,128)}, bf16[2,2,784,256]{3,2,1,0:T(8,128)(2,1)S(1)}, bf16[576,128]{1,0:T(8,128)(2,1)}) custom-call(bf16[640,128]{1,0:T(8,128)(2,1)S(1)} %bitcast.50, f32[128,128]{1,0:T(8,128)S(1)} %bitcast.49, f32[128,128]{1,0:T(8,128)S(1)} %bitcast.52, f32[224,128]{1,0:T(8,128)S(1)} %bitcast.46, ...), custom_call_target="tpu_custom_call" | custom-call | tf_op jit(solution)/shard_map/pallas_call | solution.py:854
  70.8 2.6 %all-to-all-start.5 = ((bf16[32,9,2,128]{3,2,1,0:T(2,128)(2,1)}), bf16[32,9,2,128]{3,2,1,0:T(2,128)(2,1)S(1)}, u32[]{:S(2)}, u32[]{:S(2)}) async-start(bf16[32,9,2,128]{3,2,1,0:T(2,128)(2,1)} %bitcast.24), calls=%async_computation.5 | async-start | bytes 294912 | tf_op jit(solution)/shard_map/all_to_all | solution.py:812
  73.4 1.2 %copy.27 = bf16[4,14,56,256]{3,2,1,0:T(8,128)(2,1)} copy(bf16[4,14,56,256]{3,2,1,0:T(8,128)(2,1)S(1)} %bitcast.36) | data formatting | bytes 3211264
  74.6 7.3 %all-to-all-done.5 = bf16[32,9,2,128]{3,2,1,0:T(2,128)(2,1)S(1)} async-done(((bf16[32,9,2,128]{3,2,1,0:T(2,128)(2,1)}), bf16[32,9,2,128]{3,2,1,0:T(2,128)(2,1)S(1)}, u32[]{:S(2)}, u32[]{:S(2)}) %all-to-all-start.5) | async-done | bytes 147488 | tf_op jit(solution)/shard_map/all_to_all | solution.py:812
  81.8 0.8 shard_map.210
  (8 shorter events, 0.0 us)
Async XLA Ops:
  1.3 2.7 %copy-start = (bf16[4,14,56,256]{3,2,1,0:T(8,128)(2,1)S(1)}, bf16[4,14,56,256]{3,2,1,0:T(8,128)(2,1)}, u32[]{:S(2)}) copy-start(bf16[4,14,56,256]{3,2,1,0:T(8,128)(2,1)} %param.12) | copy-start | bytes 4816900
  2.7 18.0 %copy-start.2 = (bf16[3,3,64,64]{3,2,1,0:T(8,128)(2,1)S(1)}, bf16[3,3,64,64]{3,2,1,0:T(8,128)(2,1)}, u32[]{:S(2)}) copy-start(bf16[3,3,64,64]{3,2,1,0:T(8,128)(2,1)} %param.14) | copy-start | bytes 221188
  2.8 18.0 %copy-start.5 = (f32[64]{0:T(128)S(1)}, f32[64]{0:T(128)}, u32[]{:S(2)}) copy-start(f32[64]{0:T(128)} %param.16) | copy-start | bytes 772
  2.8 18.0 %copy-start.8 = (f32[64]{0:T(128)S(1)}, f32[64]{0:T(128)}, u32[]{:S(2)}) copy-start(f32[64]{0:T(128)} %param.17) | copy-start | bytes 772
  2.8 17.9 %collective-permute-start = (bf16[2,2,2,112,256]{4,3,2,1,0:T(8,128)(2,1)S(1)}, bf16[2,2,2,112,256]{4,3,2,1,0:T(8,128)(2,1)S(1)}, u32[]{:S(2)}, u32[]{:S(2)}) collective-permute-start(bf16[2,2,2,112,256]{4,3,2,1,0:T(8,128)(2,1)S(1)} %get-tuple-element.54), channel_id=1, source_target_pairs={{0,1},{1,0},{2,3},{3,2},{4,5},{5,4},{6,7},{7,6},{8,9},{9,8},{10,11... | collective-permute-start | bytes 1376264 | tf_op jit(solution)/shard_map/ppermute | solution.py:885
  3.3 17.4 %collective-permute-start.1 = (bf16[2,2,2,112,256]{4,3,2,1,0:T(8,128)(2,1)S(1)}, bf16[2,2,2,112,256]{4,3,2,1,0:T(8,128)(2,1)S(1)}, u32[]{:S(2)}, u32[]{:S(2)}) collective-permute-start(bf16[2,2,2,112,256]{4,3,2,1,0:T(8,128)(2,1)S(1)} %get-tuple-element.55), channel_id=1, source_target_pairs={{1,2},{2,1},{5,6},{6,5},{9,10},{10,9},{13,14},{14,13},{17,18},{18,... | collective-permute-start | bytes 1376264 | tf_op jit(solution)/shard_map/ppermute | solution.py:886
  20.7 11.1 %copy-start.3 = (bf16[64,256]{1,0:T(8,128)(2,1)S(1)}, bf16[64,256]{1,0:T(8,128)(2,1)}, u32[]{:S(2)}) copy-start(bf16[64,256]{1,0:T(8,128)(2,1)} %expander_ref.1) | copy-start | bytes 98308
  20.7 11.1 %copy-start.4 = (f32[64]{0:T(128)S(1)}, f32[64]{0:T(128)}, u32[]{:S(2)}) copy-start(f32[64]{0:T(128)} %param.18) | copy-start | bytes 772
  20.8 11.1 %copy-start.9 = (f32[64]{0:T(128)S(1)}, f32[64]{0:T(128)}, u32[]{:S(2)}) copy-start(f32[64]{0:T(128)} %param.19) | copy-start | bytes 772
  20.8 22.3 %copy-start.1 = (bf16[4,14,56,256]{3,2,1,0:T(8,128)(2,1)S(1)}, bf16[4,14,56,256]{3,2,1,0:T(8,128)(2,1)}, u32[]{:S(2)}) copy-start(bf16[4,14,56,256]{3,2,1,0:T(8,128)(2,1)} %param.22) | copy-start | bytes 4816900
  20.8 22.3 %copy-start.6 = (f32[256]{0:T(256)S(1)}, f32[256]{0:T(256)}, u32[]{:S(2)}) copy-start(f32[256]{0:T(256)} %param.20) | copy-start | bytes 3076
  20.8 22.3 %copy-start.7 = (f32[256]{0:T(256)S(1)}, f32[256]{0:T(256)}, u32[]{:S(2)}) copy-start(f32[256]{0:T(256)} %param.21) | copy-start | bytes 3076
  70.8 11.0 %all-to-all-start.5 = ((bf16[32,9,2,128]{3,2,1,0:T(2,128)(2,1)}), bf16[32,9,2,128]{3,2,1,0:T(2,128)(2,1)S(1)}, u32[]{:S(2)}, u32[]{:S(2)}) async-start(bf16[32,9,2,128]{3,2,1,0:T(2,128)(2,1)} %bitcast.24), calls=%async_computation.5 | async-start | bytes 294912 | tf_op jit(solution)/shard_map/all_to_all | solution.py:812

commit v3 on v2

--- a/solution.py
+++ b/solution.py
@@ -430,6 +430,7 @@
     average, inverse, _ = merged(sizes, got_ref, sizes.rows2, numbers)
     gain, bias = twice(gain_ref[...]), twice(bias_ref[...])
     centre, tangent = swish(bias)
+    centre = 0.125 * jnp.floor(8.0 * centre + 0.5)
     diagonal(expand_ref, expander_ref[...])
     sums = (jnp.zeros((8, 128), F32),) * 3
     for g in range(pairs):

time: 83 us -> 82.9 us (level)
  no operation moved by 1% of the time
where the time goes in v3:
time: 82.9 us; the launch traced here: 82.6 us
  blocking collectives  54.7 us (66%)
  Pallas kernels  14.2 us (17%)
  waiting for transfers between devices  7.26 us (9%)
  starting transfers between devices  3.77 us (5%)
  between operations  1.46 us (2%)
  local copies, waits for them, and re-layouts  1.22 us (1%)
    all_to_all x5, blocking collectives, exchange(): return lax.all_to_all(parted, AXES, 0, 0).reshape(rows.shape)  54.7 us
    pallas_call x8, Pallas kernels, call(): pl.pallas_call(functools.partial(kernel, sizes), out_shape=outs, in_specs...  14.2 us
    all_to_all x1, waiting for transfers between devices, exchange(): return lax.all_to_all(parted, AXES, 0, 0).reshape(rows.shape)  7.26 us
    all_to_all x1, starting transfers between devices, exchange(): return lax.all_to_all(parted, AXES, 0, 0).reshape(rows.shape)  2.58 us
  transfers between devices with their start and end apart: 3, of which 1 were waited for; matrix products, arithmetic and copies ran while one was open for 1% of the time, Pallas kernels for 1%

profile of v3, /device:TPU:0, one launch (start us, length us, event | category | flops | bytes accessed | tf_op | source)
XLA Modules:
  0.0 82.6 jit_solution(18089983808586457510)
XLA Ops:
  1.3 0.0 copy-start
  1.3 1.4 %shard_map.203 = (bf16[128,512]{1,0:T(8,128)(2,1)S(1)}, f32[16,256]{1,0:T(8,128)S(1)}, bf16[2,2,2,112,256]{4,3,2,1,0:T(8,128)(2,1)S(1)}, bf16[2,2,2,112,256]{4,3,2,1,0:T(8,128)(2,1)S(1)}) custom-call(bf16[2,2,784,256]{3,2,1,0:T(8,128)(2,1)} %bitcast.37, bf16[2,2,784,256]{3,2,1,0:T(8,128)(2,1)} %bitcast.42, bf16[64,256]{1,0:T(8,128)(2,1)} %bitcast.70, ...), custom_call_target="tpu_custom_call" | custom-call | tf_op jit(solution)/shard_map/pallas_call | solution.py:855
  2.7 0.0 copy-start.2
  2.8 0.0 copy-start.5
  2.8 0.0 copy-start.8
  2.8 0.5 collective-permute-start
  3.3 0.7 collective-permute-start.1
  4.0 0.8 shard_map.204
  4.8 15.9 %all_to_all.30 = f32[32,4,1,128]{3,1,2,0:T(4,128)S(1)} all-to-all(f32[32,4,1,128]{3,1,2,0:T(4,128)S(1)} %bitcast.61), channel_id=1, replica_groups=mesh['img'=8,'ha'=4] {'img','ha'}, dimensions={0} | all-to-all | bytes 131072 | tf_op jit(solution)/shard_map/all_to_all | solution.py:813
  20.7 0.0 collective-permute-done.near_ref
  20.7 0.0 collective-permute-done.1.far_ref
  20.7 0.0 copy-done.5
  20.7 0.0 copy-done.8
  20.7 0.0 copy-start.3
  20.7 0.0 copy-start.4
  20.8 0.0 copy-start.9
  20.8 0.0 copy-start.1
  20.8 0.0 copy-start.6
  20.8 0.0 copy-start.7
  20.8 1.9 %shard_map.205 = (bf16[2,784,384]{2,1,0:T(8,128)(2,1)S(1)}, f32[2,784,128]{2,1,0:T(8,128)S(1)}, f32[2,896,128]{2,1,0:T(8,128)S(1)}, f32[8,128]{1,0:T(8,128)S(1)}...) custom-call(f32[128,128]{1,0:T(8,128)S(1)} %bitcast.47, bf16[2,2,784,256]{3,2,1,0:T(8,128)(2,1)S(1)} %bitcast.39, ...), custom_call_target="tpu_custom_call" | custom-call | tf_op jit(solution)/shard_map/pallas_call | solution.py:855
  22.7 9.1 %all_to_all.31 = f32[32,4,1,128]{3,1,2,0:T(4,128)S(1)} all-to-all(f32[32,4,1,128]{3,1,2,0:T(4,128)S(1)} %bitcast.60), channel_id=1, replica_groups=mesh['img'=8,'ha'=4] {'img','ha'}, dimensions={0} | all-to-all | bytes 131072 | tf_op jit(solution)/shard_map/all_to_all | solution.py:813
  31.8 1.5 %shard_map.206 = (bf16[2,896,128]{2,1,0:T(8,128)(2,1)S(1)}, f32[2,896,128]{2,1,0:T(8,128)S(1)}, f32[8,128]{1,0:T(8,128)S(1)}, f32[64,128]{1,0:T(8,128)S(1)}, bf1...) custom-call(f32[128,128]{1,0:T(8,128)S(1)} %bitcast.51, f32[128,128]{1,0:T(8,128)S(1)} %bitcast.48, ...), custom_call_target="tpu_custom_call" | custom-call | tf_op jit(solution)/shard_map/pallas_call | solution.py:855
  33.3 9.7 %all_to_all.32 = f32[32,7,1,128]{3,2,1,0:T(1,128)S(1)} all-to-all(f32[32,7,1,128]{3,2,1,0:T(1,128)S(1)} %bitcast.59), channel_id=1, replica_groups=mesh['img'=8,'ha'=4] {'img','ha'}, dimensions={0} | all-to-all | bytes 229376 | tf_op jit(solution)/shard_map/all_to_all | solution.py:813
  43.1 3.0 %shard_map.207 = (bf16[3136,256]{1,0:T(8,128)(2,1)S(1)}, f32[3136,256]{1,0:T(8,128)S(1)}, f32[2,896,128]{2,1,0:T(8,128)S(1)}, f32[8,256]{1,0:T(8,128)S(1)}, f32[...) custom-call(f32[224,128]{1,0:T(8,128)S(1)} %bitcast.44, f32[8,128]{1,0:T(8,128)S(1)} %get-tuple-element.60.norm_one_ref, ...), custom_call_target="tpu_custom_call" | custom-call | tf_op jit(solution)/shard_map/pallas_call | solution.py:855
  46.1 9.7 %all_to_all.33 = f32[32,7,1,128]{3,2,1,0:T(1,128)S(1)} all-to-all(f32[32,7,1,128]{3,2,1,0:T(1,128)S(1)} %bitcast.58), channel_id=1, replica_groups=mesh['img'=8,'ha'=4] {'img','ha'}, dimensions={0} | all-to-all | bytes 229376 | tf_op jit(solution)/shard_map/all_to_all | solution.py:813
  55.8 3.7 %shard_map.208 = (f32[1,256]{1,0:T(1,128)}, f32[1,256]{1,0:T(1,128)}, f32[1,64]{1,0:T(1,128)}, f32[1,64]{1,0:T(1,128)}, f32[2,784,128]{2,1,0:T(8,128)S(1)}, /*in...) custom-call(f32[224,128]{1,0:T(8,128)S(1)} %bitcast.56, f32[224,128]{1,0:T(8,128)S(1)} %bitcast.45, ...), custom_call_target="tpu_custom_call" | custom-call | tf_op jit(solution)/shard_map/pallas_call | solution.py:855
  59.5 10.3 %all_to_all.34 = bf16[32,10,2,128]{3,2,1,0:T(2,128)(2,1)S(1)} all-to-all(bf16[32,10,2,128]{3,2,1,0:T(2,128)(2,1)S(1)} %bitcast.57), channel_id=1, replica_groups=mesh['img'=8,'ha'=4] {'img','ha'}, dimensions={0} | all-to-all | bytes 327680 | tf_op jit(solution)/shard_map/all_to_all | solution.py:813
  69.8 1.0 %shard_map.209 = (f32[1,64]{1,0:T(1,128)}, f32[1,64]{1,0:T(1,128)}, bf16[2,2,784,256]{3,2,1,0:T(8,128)(2,1)S(1)}, bf16[576,128]{1,0:T(8,128)(2,1)}) custom-call(bf16[640,128]{1,0:T(8,128)(2,1)S(1)} %bitcast.50, f32[128,128]{1,0:T(8,128)S(1)} %bitcast.49, f32[128,128]{1,0:T(8,128)S(1)} %bitcast.52, f32[224,128]{1,0:T(8,128)S(1)} %bitcast.46, ...), custom_call_target="tpu_custom_call" | custom-call | tf_op jit(solution)/shard_map/pallas_call | solution.py:855
  70.8 2.6 %all-to-all-start.5 = ((bf16[32,9,2,128]{3,2,1,0:T(2,128)(2,1)}), bf16[32,9,2,128]{3,2,1,0:T(2,128)(2,1)S(1)}, u32[]{:S(2)}, u32[]{:S(2)}) async-start(bf16[32,9,2,128]{3,2,1,0:T(2,128)(2,1)} %bitcast.24), calls=%async_computation.5 | async-start | bytes 294912 | tf_op jit(solution)/shard_map/all_to_all | solution.py:813
  73.4 1.2 %copy.27 = bf16[4,14,56,256]{3,2,1,0:T(8,128)(2,1)} copy(bf16[4,14,56,256]{3,2,1,0:T(8,128)(2,1)S(1)} %bitcast.36) | data formatting | bytes 3211264
  74.6 7.3 %all-to-all-done.5 = bf16[32,9,2,128]{3,2,1,0:T(2,128)(2,1)S(1)} async-done(((bf16[32,9,2,128]{3,2,1,0:T(2,128)(2,1)}), bf16[32,9,2,128]{3,2,1,0:T(2,128)(2,1)S(1)}, u32[]{:S(2)}, u32[]{:S(2)}) %all-to-all-start.5) | async-done | bytes 147488 | tf_op jit(solution)/shard_map/all_to_all | solution.py:813
  81.8 0.8 shard_map.210
  (8 shorter events, 0.0 us)
Async XLA Ops:
  1.3 2.7 %copy-start = (bf16[4,14,56,256]{3,2,1,0:T(8,128)(2,1)S(1)}, bf16[4,14,56,256]{3,2,1,0:T(8,128)(2,1)}, u32[]{:S(2)}) copy-start(bf16[4,14,56,256]{3,2,1,0:T(8,128)(2,1)} %param.12) | copy-start | bytes 4816900
  2.7 18.0 %copy-start.2 = (bf16[3,3,64,64]{3,2,1,0:T(8,128)(2,1)S(1)}, bf16[3,3,64,64]{3,2,1,0:T(8,128)(2,1)}, u32[]{:S(2)}) copy-start(bf16[3,3,64,64]{3,2,1,0:T(8,128)(2,1)} %param.14) | copy-start | bytes 221188
  2.8 18.0 %copy-start.5 = (f32[64]{0:T(128)S(1)}, f32[64]{0:T(128)}, u32[]{:S(2)}) copy-start(f32[64]{0:T(128)} %param.16) | copy-start | bytes 772
  2.8 18.0 %copy-start.8 = (f32[64]{0:T(128)S(1)}, f32[64]{0:T(128)}, u32[]{:S(2)}) copy-start(f32[64]{0:T(128)} %param.17) | copy-start | bytes 772
  2.8 17.9 %collective-permute-start = (bf16[2,2,2,112,256]{4,3,2,1,0:T(8,128)(2,1)S(1)}, bf16[2,2,2,112,256]{4,3,2,1,0:T(8,128)(2,1)S(1)}, u32[]{:S(2)}, u32[]{:S(2)}) collective-permute-start(bf16[2,2,2,112,256]{4,3,2,1,0:T(8,128)(2,1)S(1)} %get-tuple-element.54), channel_id=1, source_target_pairs={{0,1},{1,0},{2,3},{3,2},{4,5},{5,4},{6,7},{7,6},{8,9},{9,8},{10,11... | collective-permute-start | bytes 1376264 | tf_op jit(solution)/shard_map/ppermute | solution.py:886
  3.3 17.4 %collective-permute-start.1 = (bf16[2,2,2,112,256]{4,3,2,1,0:T(8,128)(2,1)S(1)}, bf16[2,2,2,112,256]{4,3,2,1,0:T(8,128)(2,1)S(1)}, u32[]{:S(2)}, u32[]{:S(2)}) collective-permute-start(bf16[2,2,2,112,256]{4,3,2,1,0:T(8,128)(2,1)S(1)} %get-tuple-element.55), channel_id=1, source_target_pairs={{1,2},{2,1},{5,6},{6,5},{9,10},{10,9},{13,14},{14,13},{17,18},{18,... | collective-permute-start | bytes 1376264 | tf_op jit(solution)/shard_map/ppermute | solution.py:887
  20.7 11.1 %copy-start.3 = (bf16[64,256]{1,0:T(8,128)(2,1)S(1)}, bf16[64,256]{1,0:T(8,128)(2,1)}, u32[]{:S(2)}) copy-start(bf16[64,256]{1,0:T(8,128)(2,1)} %expander_ref.1) | copy-start | bytes 98308
  20.7 11.1 %copy-start.4 = (f32[64]{0:T(128)S(1)}, f32[64]{0:T(128)}, u32[]{:S(2)}) copy-start(f32[64]{0:T(128)} %param.18) | copy-start | bytes 772
  20.8 11.1 %copy-start.9 = (f32[64]{0:T(128)S(1)}, f32[64]{0:T(128)}, u32[]{:S(2)}) copy-start(f32[64]{0:T(128)} %param.19) | copy-start | bytes 772
  20.8 22.3 %copy-start.1 = (bf16[4,14,56,256]{3,2,1,0:T(8,128)(2,1)S(1)}, bf16[4,14,56,256]{3,2,1,0:T(8,128)(2,1)}, u32[]{:S(2)}) copy-start(bf16[4,14,56,256]{3,2,1,0:T(8,128)(2,1)} %param.22) | copy-start | bytes 4816900
  20.8 22.3 %copy-start.6 = (f32[256]{0:T(256)S(1)}, f32[256]{0:T(256)}, u32[]{:S(2)}) copy-start(f32[256]{0:T(256)} %param.20) | copy-start | bytes 3076
  20.8 22.3 %copy-start.7 = (f32[256]{0:T(256)S(1)}, f32[256]{0:T(256)}, u32[]{:S(2)}) copy-start(f32[256]{0:T(256)} %param.21) | copy-start | bytes 3076
  70.8 11.0 %all-to-all-start.5 = ((bf16[32,9,2,128]{3,2,1,0:T(2,128)(2,1)}), bf16[32,9,2,128]{3,2,1,0:T(2,128)(2,1)S(1)}, u32[]{:S(2)}, u32[]{:S(2)}) async-start(bf16[32,9,2,128]{3,2,1,0:T(2,128)(2,1)} %bitcast.24), calls=%async_computation.5 | async-start | bytes 294912 | tf_op jit(solution)/shard_map/all_to_all | solution.py:813

commit v4 on v3

--- a/solution.py
+++ b/solution.py
@@ -163,6 +163,7 @@
         self.chunks = height // 2
         self.ext = self.own + self.step
         self.sample = 32
+        self.edge = -(-across // 16) * 16
         self.wide1 = (height + 4) * across
         self.wide2 = (height + 2) * across
         self.share = max(1, 64 // count)
@@ -265,12 +266,12 @@
     step, own = sizes.step, sizes.own
     edges = []
     odd = lax.rem(lax.axis_index("ha"), 2)
-    to_last = pl.multiple_of((1 - odd) * (own - step), step)
-    to_head = pl.multiple_of(odd * (own - step), step)
-    for out, start in ((near_ref, to_last), (far_ref, to_head)):
-        for place, source in enumerate((feat_hbm, up_hbm)):
+    edge = sizes.edge
+    for out, last in ((near_ref, 1 - odd), (far_ref, odd)):
+        for source, size, place in ((feat_hbm, step, 0), (up_hbm, edge, step)):
+            start = pl.multiple_of(last * (own - size), 16)
             copy = pltpu.make_async_copy(
-                source.at[:, :, pl.ds(start, step), :], out.at[place], sem_ref.at[len(edges)]
+                source.at[:, :, pl.ds(start, size), :], out.at[:, :, pl.ds(place, size), :], sem_ref.at[len(edges)]
             )
             copy.start()
             edges.append(copy)
@@ -351,7 +352,7 @@
 
         lax.fori_loop(0, sizes.chunks, activate, 0, unroll=True)
         for start, valid, rows_ref in ((near_start, 1.0, near_ref), (far_start, has_far, far_ref)):
-            low, high = rows_ref[0, 0, g], rows_ref[0, 1, g]
+            low, high = rows_ref[0, g, 0:step, :], rows_ref[1, g, 0:step, :]
             first = nt(jnp.concatenate([low, high], axis=1), weight_ref[...])
             value, _ = swish((first - average) * inverse * gain + bias)
             value = value * valid
@@ -485,7 +486,7 @@
 def output_kernel(
     sizes, got_ref, norm_one_ref, norm_ref, hidden_ref, slope_ref, second_ref, feat_ref, up_ref,
     near_ref, far_ref, gain_ref, bias_ref, expand_ref, real_ref,
-    active_ref, gsum_ref, back_ref, last_ref, raw_ref, out_ref, scaled_ref,
+    active_ref, gsum_ref, back_ref, last_ref, raw_ref, out_ref, scaled_ref, third_ref,
 ):
     pairs, step, own, across = sizes.pairs, sizes.step, sizes.own, sizes.across
     odd = lax.rem(lax.axis_index("ha"), 2) == 1
@@ -525,11 +526,12 @@
         valids = [image_mask(sizes, real_ref, g + half * pairs) for half in range(2)]
         middles = [middle * valid for valid in valids]
 
+        third_ref[g * own : (g + 1) * own, :] = nn(hidden_ref[g, 0:own, :], expand_ref[...])
+
         def body(c, biases):
-            hidden = hidden_ref[g, block(c * step, step), :]
             for half in range(2):
                 image = g + half * pairs
-                third = nn(hidden, expand_ref[:, half * 256 : (half + 1) * 256])
+                third = third_ref[block(g * own + c * step, step), half * 256 : (half + 1) * 256]
                 for start in range(0, step, 16):
                     here = pl.ds(pl.multiple_of(c * step + start, 16), 16)
                     place = pl.ds(pl.multiple_of(image * own + c * step + start, 16), 16)
@@ -549,10 +551,10 @@
         for half in range(2):
             image = g + half * pairs
             both = []
-            for which in range(2):
-                near = near_ref[which, half, g].astype(F32)
-                far = far_ref[which, half, g].astype(F32)
-                upper = jnp.where(odd, near[across:, :], far[across:, :])
+            for start, size in ((0, step), (step, sizes.edge)):
+                near = near_ref[half, g, start : start + size, :].astype(F32)
+                far = far_ref[half, g, start : start + size, :].astype(F32)
+                upper = jnp.where(odd, near[size - across :, :], far[size - across :, :])
                 lower = jnp.where(odd, far[0:across, :], near[0:across, :])
                 both.append(jnp.concatenate([upper, lower], axis=0))
             _, slope = outward(nn(hidden, expand_ref[:, half * 256 : (half + 1) * 256]), both[0])
@@ -876,8 +878,8 @@
         (
             shape(128, 512, dtype=BF16),
             shape(16, 256),
-            shape(2, 2, pairs, step, wide, dtype=BF16),
-            shape(2, 2, pairs, step, wide, dtype=BF16),
+            shape(2, pairs, step + sizes.edge, wide, dtype=BF16),
+            shape(2, pairs, step + sizes.edge, wide, dtype=BF16),
         ),
         (*given, image_counts),
         [pltpu.VMEM((64, 256), BF16), pltpu.SemaphoreType.DMA((5,))],
@@ -934,7 +936,7 @@
             got3, norm_one, norm_two, hidden_two, slope_two, second, feat, up_hbm, near_rows, far_rows,
             gain3, bias3, expand, real,
         ),
-        [pltpu.VMEM((pairs * sizes.ext, 2 * wide), BF16)],
+        [pltpu.VMEM((pairs * sizes.ext, 2 * wide), BF16), pltpu.VMEM((pairs * own, 2 * wide), F32)],
     )
     got4 = exchange(rows, count)
     gradgain3, gradbias3, gradgain2, gradbias2, grad_one, activated, rows = call(

time: 82.9 us -> 82.8 us (level)
  no operation moved by 1% of the time
where the time goes in v4:
time: 82.8 us; the launch traced here: 82.5 us
  blocking collectives  54.7 us (66%)
  Pallas kernels  14.1 us (17%)
  waiting for transfers between devices  7.26 us (9%)
  starting transfers between devices  3.77 us (5%)
  between operations  1.46 us (2%)
  local copies, waits for them, and re-layouts  1.22 us (1%)
    all_to_all x5, blocking collectives, exchange(): return lax.all_to_all(parted, AXES, 0, 0).reshape(rows.shape)  54.7 us
    pallas_call x8, Pallas kernels, call(): pl.pallas_call(functools.partial(kernel, sizes), out_shape=outs, in_specs...  14.1 us
    all_to_all x1, waiting for transfers between devices, exchange(): return lax.all_to_all(parted, AXES, 0, 0).reshape(rows.shape)  7.26 us
    all_to_all x1, starting transfers between devices, exchange(): return lax.all_to_all(parted, AXES, 0, 0).reshape(rows.shape)  2.58 us
  transfers between devices with their start and end apart: 3, of which 1 were waited for; matrix products, arithmetic and copies ran while one was open for 1% of the time, Pallas kernels for 1%

profile of v4, /device:TPU:0, one launch (start us, length us, event | category | flops | bytes accessed | tf_op | source)
XLA Modules:
  0.0 82.5 jit_solution(9221395394830118253)
XLA Ops:
  1.3 1.4 %shard_map.203 = (bf16[128,512]{1,0:T(8,128)(2,1)S(1)}, f32[16,256]{1,0:T(8,128)S(1)}, bf16[2,2,176,256]{3,2,1,0:T(8,128)(2,1)S(1)}, bf16[2,2,176,256]{3,2,1,0:T(8,128)(2,1)S(1)}) custom-call(bf16[2,2,784,256]{3,2,1,0:T(8,128)(2,1)} %bitcast.37, bf16[2,2,784,256]{3,2,1,0:T(8,128)(2,1)} %bitcast.42, bf16[64,256]{1,0:T(8,128)(2,1)} %bitcast.70, ...), custom_call_target="tpu_custom_call" | custom-call | tf_op jit(solution)/shard_map/pallas_call | solution.py:857
  2.7 0.0 copy-start.2
  2.7 0.0 copy-start.5
  2.7 0.0 copy-start.8
  2.7 0.5 collective-permute-start
  3.2 0.7 collective-permute-start.1
  3.9 0.0 copy-done
  3.9 0.8 shard_map.204
  4.7 15.9 %all_to_all.30 = f32[32,4,1,128]{3,1,2,0:T(4,128)S(1)} all-to-all(f32[32,4,1,128]{3,1,2,0:T(4,128)S(1)} %bitcast.61), channel_id=1, replica_groups=mesh['img'=8,'ha'=4] {'img','ha'}, dimensions={0} | all-to-all | bytes 131072 | tf_op jit(solution)/shard_map/all_to_all | solution.py:815
  20.6 0.0 collective-permute-done.near_ref
  20.6 0.0 collective-permute-done.1.far_ref
  20.6 0.0 copy-done.2
  20.7 0.0 copy-start.3
  20.7 0.0 copy-start.4
  20.7 0.0 copy-start.9
  20.7 0.0 copy-start.1
  20.7 0.0 copy-start.6
  20.7 0.0 copy-start.7
  20.7 1.9 %shard_map.205 = (bf16[2,784,384]{2,1,0:T(8,128)(2,1)S(1)}, f32[2,784,128]{2,1,0:T(8,128)S(1)}, f32[2,896,128]{2,1,0:T(8,128)S(1)}, f32[8,128]{1,0:T(8,128)S(1)}...) custom-call(f32[128,128]{1,0:T(8,128)S(1)} %bitcast.47, bf16[2,2,784,256]{3,2,1,0:T(8,128)(2,1)S(1)} %bitcast.39, ...), custom_call_target="tpu_custom_call" | custom-call | tf_op jit(solution)/shard_map/pallas_call | solution.py:857
  22.6 9.1 %all_to_all.31 = f32[32,4,1,128]{3,1,2,0:T(4,128)S(1)} all-to-all(f32[32,4,1,128]{3,1,2,0:T(4,128)S(1)} %bitcast.60), channel_id=1, replica_groups=mesh['img'=8,'ha'=4] {'img','ha'}, dimensions={0} | all-to-all | bytes 131072 | tf_op jit(solution)/shard_map/all_to_all | solution.py:815
  31.7 0.0 copy-done.4
  31.8 1.5 %shard_map.206 = (bf16[2,896,128]{2,1,0:T(8,128)(2,1)S(1)}, f32[2,896,128]{2,1,0:T(8,128)S(1)}, f32[8,128]{1,0:T(8,128)S(1)}, f32[64,128]{1,0:T(8,128)S(1)}, bf1...) custom-call(f32[128,128]{1,0:T(8,128)S(1)} %bitcast.51, f32[128,128]{1,0:T(8,128)S(1)} %bitcast.48, ...), custom_call_target="tpu_custom_call" | custom-call | tf_op jit(solution)/shard_map/pallas_call | solution.py:857
  33.3 9.7 %all_to_all.32 = f32[32,7,1,128]{3,2,1,0:T(1,128)S(1)} all-to-all(f32[32,7,1,128]{3,2,1,0:T(1,128)S(1)} %bitcast.59), channel_id=1, replica_groups=mesh['img'=8,'ha'=4] {'img','ha'}, dimensions={0} | all-to-all | bytes 229376 | tf_op jit(solution)/shard_map/all_to_all | solution.py:815
  43.0 3.0 %shard_map.207 = (bf16[3136,256]{1,0:T(8,128)(2,1)S(1)}, f32[3136,256]{1,0:T(8,128)S(1)}, f32[2,896,128]{2,1,0:T(8,128)S(1)}, f32[8,256]{1,0:T(8,128)S(1)}, f32[...) custom-call(f32[224,128]{1,0:T(8,128)S(1)} %bitcast.44, f32[8,128]{1,0:T(8,128)S(1)} %get-tuple-element.60.norm_one_ref, ...), custom_call_target="tpu_custom_call" | custom-call | tf_op jit(solution)/shard_map/pallas_call | solution.py:857
  46.0 9.7 %all_to_all.33 = f32[32,7,1,128]{3,2,1,0:T(1,128)S(1)} all-to-all(f32[32,7,1,128]{3,2,1,0:T(1,128)S(1)} %bitcast.58), channel_id=1, replica_groups=mesh['img'=8,'ha'=4] {'img','ha'}, dimensions={0} | all-to-all | bytes 229376 | tf_op jit(solution)/shard_map/all_to_all | solution.py:815
  55.7 3.7 %shard_map.208 = (f32[1,256]{1,0:T(1,128)}, f32[1,256]{1,0:T(1,128)}, f32[1,64]{1,0:T(1,128)}, f32[1,64]{1,0:T(1,128)}, f32[2,784,128]{2,1,0:T(8,128)S(1)}, /*in...) custom-call(f32[224,128]{1,0:T(8,128)S(1)} %bitcast.56, f32[224,128]{1,0:T(8,128)S(1)} %bitcast.45, ...), custom_call_target="tpu_custom_call" | custom-call | tf_op jit(solution)/shard_map/pallas_call | solution.py:857
  59.4 10.3 %all_to_all.34 = bf16[32,10,2,128]{3,2,1,0:T(2,128)(2,1)S(1)} all-to-all(bf16[32,10,2,128]{3,2,1,0:T(2,128)(2,1)S(1)} %bitcast.57), channel_id=1, replica_groups=mesh['img'=8,'ha'=4] {'img','ha'}, dimensions={0} | all-to-all | bytes 327680 | tf_op jit(solution)/shard_map/all_to_all | solution.py:815
  69.6 1.0 %shard_map.209 = (f32[1,64]{1,0:T(1,128)}, f32[1,64]{1,0:T(1,128)}, bf16[2,2,784,256]{3,2,1,0:T(8,128)(2,1)S(1)}, bf16[576,128]{1,0:T(8,128)(2,1)}) custom-call(bf16[640,128]{1,0:T(8,128)(2,1)S(1)} %bitcast.50, f32[128,128]{1,0:T(8,128)S(1)} %bitcast.49, f32[128,128]{1,0:T(8,128)S(1)} %bitcast.52, f32[224,128]{1,0:T(8,128)S(1)} %bitcast.46, ...), custom_call_target="tpu_custom_call" | custom-call | tf_op jit(solution)/shard_map/pallas_call | solution.py:857
  70.7 2.6 %all-to-all-start.5 = ((bf16[32,9,2,128]{3,2,1,0:T(2,128)(2,1)}), bf16[32,9,2,128]{3,2,1,0:T(2,128)(2,1)S(1)}, u32[]{:S(2)}, u32[]{:S(2)}) async-start(bf16[32,9,2,128]{3,2,1,0:T(2,128)(2,1)} %bitcast.24), calls=%async_computation.5 | async-start | bytes 294912 | tf_op jit(solution)/shard_map/all_to_all | solution.py:815
  73.2 1.2 %copy.27 = bf16[4,14,56,256]{3,2,1,0:T(8,128)(2,1)} copy(bf16[4,14,56,256]{3,2,1,0:T(8,128)(2,1)S(1)} %bitcast.36) | data formatting | bytes 3211264
  74.4 7.3 %all-to-all-done.5 = bf16[32,9,2,128]{3,2,1,0:T(2,128)(2,1)S(1)} async-done(((bf16[32,9,2,128]{3,2,1,0:T(2,128)(2,1)}), bf16[32,9,2,128]{3,2,1,0:T(2,128)(2,1)S(1)}, u32[]{:S(2)}, u32[]{:S(2)}) %all-to-all-start.5) | async-done | bytes 147488 | tf_op jit(solution)/shard_map/all_to_all | solution.py:815
  81.7 0.8 %shard_map.210 = (f32[64,256]{1,0:T(8,128)}, f32[64,256]{1,0:T(8,128)}, f32[576,64]{1,0:T(8,128)}) custom-call(bf16[576,128]{1,0:T(8,128)(2,1)S(1)} %bitcast.53), custom_call_target="tpu_custom_call" | custom-call | tf_op jit(solution)/shard_map/pallas_call | solution.py:857
  (8 shorter events, 0.0 us)
Async XLA Ops:
  1.3 2.6 %copy-start = (bf16[4,14,56,256]{3,2,1,0:T(8,128)(2,1)S(1)}, bf16[4,14,56,256]{3,2,1,0:T(8,128)(2,1)}, u32[]{:S(2)}) copy-start(bf16[4,14,56,256]{3,2,1,0:T(8,128)(2,1)} %param.12) | copy-start | bytes 4816900
  2.7 18.0 %copy-start.2 = (bf16[3,3,64,64]{3,2,1,0:T(8,128)(2,1)S(1)}, bf16[3,3,64,64]{3,2,1,0:T(8,128)(2,1)}, u32[]{:S(2)}) copy-start(bf16[3,3,64,64]{3,2,1,0:T(8,128)(2,1)} %param.14) | copy-start | bytes 221188
  2.7 18.0 %copy-start.5 = (f32[64]{0:T(128)S(1)}, f32[64]{0:T(128)}, u32[]{:S(2)}) copy-start(f32[64]{0:T(128)} %param.16) | copy-start | bytes 772
  2.7 18.0 %copy-start.8 = (f32[64]{0:T(128)S(1)}, f32[64]{0:T(128)}, u32[]{:S(2)}) copy-start(f32[64]{0:T(128)} %param.17) | copy-start | bytes 772
  2.7 17.9 %collective-permute-start = (bf16[2,2,176,256]{3,2,1,0:T(8,128)(2,1)S(1)}, bf16[2,2,176,256]{3,2,1,0:T(8,128)(2,1)S(1)}, u32[]{:S(2)}, u32[]{:S(2)}) collective-permute-start(bf16[2,2,176,256]{3,2,1,0:T(8,128)(2,1)S(1)} %get-tuple-element.54), channel_id=1, source_target_pairs={{0,1},{1,0},{2,3},{3,2},{4,5},{5,4},{6,7},{7,6},{8,9},{9,8},{10,11... | collective-permute-start | bytes 1081352 | tf_op jit(solution)/shard_map/ppermute | solution.py:888
  3.2 17.4 %collective-permute-start.1 = (bf16[2,2,176,256]{3,2,1,0:T(8,128)(2,1)S(1)}, bf16[2,2,176,256]{3,2,1,0:T(8,128)(2,1)S(1)}, u32[]{:S(2)}, u32[]{:S(2)}) collective-permute-start(bf16[2,2,176,256]{3,2,1,0:T(8,128)(2,1)S(1)} %get-tuple-element.55), channel_id=1, source_target_pairs={{1,2},{2,1},{5,6},{6,5},{9,10},{10,9},{13,14},{14,13},{17,18},{18,... | collective-permute-start | bytes 1081352 | tf_op jit(solution)/shard_map/ppermute | solution.py:889
  20.7 11.1 %copy-start.3 = (bf16[64,256]{1,0:T(8,128)(2,1)S(1)}, bf16[64,256]{1,0:T(8,128)(2,1)}, u32[]{:S(2)}) copy-start(bf16[64,256]{1,0:T(8,128)(2,1)} %expander_ref.1) | copy-start | bytes 98308
  20.7 11.1 %copy-start.4 = (f32[64]{0:T(128)S(1)}, f32[64]{0:T(128)}, u32[]{:S(2)}) copy-start(f32[64]{0:T(128)} %param.18) | copy-start | bytes 772
  20.7 11.1 %copy-start.9 = (f32[64]{0:T(128)S(1)}, f32[64]{0:T(128)}, u32[]{:S(2)}) copy-start(f32[64]{0:T(128)} %param.19) | copy-start | bytes 772
  20.7 22.3 %copy-start.1 = (bf16[4,14,56,256]{3,2,1,0:T(8,128)(2,1)S(1)}, bf16[4,14,56,256]{3,2,1,0:T(8,128)(2,1)}, u32[]{:S(2)}) copy-start(bf16[4,14,56,256]{3,2,1,0:T(8,128)(2,1)} %param.22) | copy-start | bytes 4816900
  20.7 22.3 %copy-start.6 = (f32[256]{0:T(256)S(1)}, f32[256]{0:T(256)}, u32[]{:S(2)}) copy-start(f32[256]{0:T(256)} %param.20) | copy-start | bytes 3076
  20.7 22.3 %copy-start.7 = (f32[256]{0:T(256)S(1)}, f32[256]{0:T(256)}, u32[]{:S(2)}) copy-start(f32[256]{0:T(256)} %param.21) | copy-start | bytes 3076
  70.7 11.0 %all-to-all-start.5 = ((bf16[32,9,2,128]{3,2,1,0:T(2,128)(2,1)}), bf16[32,9,2,128]{3,2,1,0:T(2,128)(2,1)S(1)}, u32[]{:S(2)}, u32[]{:S(2)}) async-start(bf16[32,9,2,128]{3,2,1,0:T(2,128)(2,1)} %bitcast.24), calls=%async_computation.5 | async-start | bytes 294912 | tf_op jit(solution)/shard_map/all_to_all | solution.py:815

commit v5 on v3

--- a/solution.py
+++ b/solution.py
@@ -485,7 +485,7 @@
 def output_kernel(
     sizes, got_ref, norm_one_ref, norm_ref, hidden_ref, slope_ref, second_ref, feat_ref, up_ref,
     near_ref, far_ref, gain_ref, bias_ref, expand_ref, real_ref,
-    active_ref, gsum_ref, back_ref, last_ref, raw_ref, out_ref, scaled_ref,
+    active_ref, gsum_ref, back_ref, last_ref, raw_ref, out_ref, scaled_ref, third_ref,
 ):
     pairs, step, own, across = sizes.pairs, sizes.step, sizes.own, sizes.across
     odd = lax.rem(lax.axis_index("ha"), 2) == 1
@@ -525,11 +525,12 @@
         valids = [image_mask(sizes, real_ref, g + half * pairs) for half in range(2)]
         middles = [middle * valid for valid in valids]
 
+        third_ref[g * own : (g + 1) * own, :] = nn(hidden_ref[g, 0:own, :], expand_ref[...])
+
         def body(c, biases):
-            hidden = hidden_ref[g, block(c * step, step), :]
             for half in range(2):
                 image = g + half * pairs
-                third = nn(hidden, expand_ref[:, half * 256 : (half + 1) * 256])
+                third = third_ref[block(g * own + c * step, step), half * 256 : (half + 1) * 256]
                 for start in range(0, step, 16):
                     here = pl.ds(pl.multiple_of(c * step + start, 16), 16)
                     place = pl.ds(pl.multiple_of(image * own + c * step + start, 16), 16)
@@ -934,7 +935,7 @@
             got3, norm_one, norm_two, hidden_two, slope_two, second, feat, up_hbm, near_rows, far_rows,
             gain3, bias3, expand, real,
         ),
-        [pltpu.VMEM((pairs * sizes.ext, 2 * wide), BF16)],
+        [pltpu.VMEM((pairs * sizes.ext, 2 * wide), BF16), pltpu.VMEM((pairs * own, 2 * wide), F32)],
     )
     got4 = exchange(rows, count)
     gradgain3, gradbias3, gradgain2, gradbias2, grad_one, activated, rows = call(

time: 82.9 us -> 82.9 us (level)
  no operation moved by 1% of the time
where the time goes in v5:
time: 82.9 us; the launch traced here: 82.6 us
  blocking collectives  54.7 us (66%)
  Pallas kernels  14.2 us (17%)
  waiting for transfers between devices  7.26 us (9%)
  starting transfers between devices  3.77 us (5%)
  between operations  1.46 us (2%)
  local copies, waits for them, and re-layouts  1.22 us (1%)
    all_to_all x5, blocking collectives, exchange(): return lax.all_to_all(parted, AXES, 0, 0).reshape(rows.shape)  54.7 us
    pallas_call x8, Pallas kernels, call(): pl.pallas_call(functools.partial(kernel, sizes), out_shape=outs, in_specs...  14.2 us
    all_to_all x1, waiting for transfers between devices, exchange(): return lax.all_to_all(parted, AXES, 0, 0).reshape(rows.shape)  7.26 us
    all_to_all x1, starting transfers between devices, exchange(): return lax.all_to_all(parted, AXES, 0, 0).reshape(rows.shape)  2.58 us
  transfers between devices with their start and end apart: 3, of which 1 were waited for; matrix products, arithmetic and copies ran while one was open for 1% of the time, Pallas kernels for 1%

profile of v5, /device:TPU:0, one launch (start us, length us, event | category | flops | bytes accessed | tf_op | source)
XLA Modules:
  0.0 82.6 jit_solution(16238346353037843683)
XLA Ops:
  1.3 0.0 copy-start
  1.3 1.4 %shard_map.203 = (bf16[128,512]{1,0:T(8,128)(2,1)S(1)}, f32[16,256]{1,0:T(8,128)S(1)}, bf16[2,2,2,112,256]{4,3,2,1,0:T(8,128)(2,1)S(1)}, bf16[2,2,2,112,256]{4,3,2,1,0:T(8,128)(2,1)S(1)}) custom-call(bf16[2,2,784,256]{3,2,1,0:T(8,128)(2,1)} %bitcast.37, bf16[2,2,784,256]{3,2,1,0:T(8,128)(2,1)} %bitcast.42, bf16[64,256]{1,0:T(8,128)(2,1)} %bitcast.70, ...), custom_call_target="tpu_custom_call" | custom-call | tf_op jit(solution)/shard_map/pallas_call | solution.py:856
  2.7 0.0 copy-start.2
  2.8 0.0 copy-start.5
  2.8 0.0 copy-start.8
  2.8 0.5 collective-permute-start
  3.3 0.7 collective-permute-start.1
  4.0 0.8 shard_map.204
  4.8 15.9 %all_to_all.30 = f32[32,4,1,128]{3,1,2,0:T(4,128)S(1)} all-to-all(f32[32,4,1,128]{3,1,2,0:T(4,128)S(1)} %bitcast.61), channel_id=1, replica_groups=mesh['img'=8,'ha'=4] {'img','ha'}, dimensions={0} | all-to-all | bytes 131072 | tf_op jit(solution)/shard_map/all_to_all | solution.py:814
  20.7 0.0 collective-permute-done.near_ref
  20.7 0.0 collective-permute-done.1.far_ref
  20.7 0.0 copy-done.5
  20.7 0.0 copy-done.8
  20.7 0.0 copy-start.3
  20.7 0.0 copy-start.4
  20.8 0.0 copy-start.9
  20.8 0.0 copy-start.1
  20.8 0.0 copy-start.6
  20.8 0.0 copy-start.7
  20.8 1.9 %shard_map.205 = (bf16[2,784,384]{2,1,0:T(8,128)(2,1)S(1)}, f32[2,784,128]{2,1,0:T(8,128)S(1)}, f32[2,896,128]{2,1,0:T(8,128)S(1)}, f32[8,128]{1,0:T(8,128)S(1)}...) custom-call(f32[128,128]{1,0:T(8,128)S(1)} %bitcast.47, bf16[2,2,784,256]{3,2,1,0:T(8,128)(2,1)S(1)} %bitcast.39, ...), custom_call_target="tpu_custom_call" | custom-call | tf_op jit(solution)/shard_map/pallas_call | solution.py:856
  22.7 9.1 %all_to_all.31 = f32[32,4,1,128]{3,1,2,0:T(4,128)S(1)} all-to-all(f32[32,4,1,128]{3,1,2,0:T(4,128)S(1)} %bitcast.60), channel_id=1, replica_groups=mesh['img'=8,'ha'=4] {'img','ha'}, dimensions={0} | all-to-all | bytes 131072 | tf_op jit(solution)/shard_map/all_to_all | solution.py:814
  31.8 1.5 %shard_map.206 = (bf16[2,896,128]{2,1,0:T(8,128)(2,1)S(1)}, f32[2,896,128]{2,1,0:T(8,128)S(1)}, f32[8,128]{1,0:T(8,128)S(1)}, f32[64,128]{1,0:T(8,128)S(1)}, bf1...) custom-call(f32[128,128]{1,0:T(8,128)S(1)} %bitcast.51, f32[128,128]{1,0:T(8,128)S(1)} %bitcast.48, ...), custom_call_target="tpu_custom_call" | custom-call | tf_op jit(solution)/shard_map/pallas_call | solution.py:856
  33.3 9.7 %all_to_all.32 = f32[32,7,1,128]{3,2,1,0:T(1,128)S(1)} all-to-all(f32[32,7,1,128]{3,2,1,0:T(1,128)S(1)} %bitcast.59), channel_id=1, replica_groups=mesh['img'=8,'ha'=4] {'img','ha'}, dimensions={0} | all-to-all | bytes 229376 | tf_op jit(solution)/shard_map/all_to_all | solution.py:814
  43.1 3.0 %shard_map.207 = (bf16[3136,256]{1,0:T(8,128)(2,1)S(1)}, f32[3136,256]{1,0:T(8,128)S(1)}, f32[2,896,128]{2,1,0:T(8,128)S(1)}, f32[8,256]{1,0:T(8,128)S(1)}, f32[...) custom-call(f32[224,128]{1,0:T(8,128)S(1)} %bitcast.44, f32[8,128]{1,0:T(8,128)S(1)} %get-tuple-element.60.norm_one_ref, ...), custom_call_target="tpu_custom_call" | custom-call | tf_op jit(solution)/shard_map/pallas_call | solution.py:856
  46.0 9.7 %all_to_all.33 = f32[32,7,1,128]{3,2,1,0:T(1,128)S(1)} all-to-all(f32[32,7,1,128]{3,2,1,0:T(1,128)S(1)} %bitcast.58), channel_id=1, replica_groups=mesh['img'=8,'ha'=4] {'img','ha'}, dimensions={0} | all-to-all | bytes 229376 | tf_op jit(solution)/shard_map/all_to_all | solution.py:814
  55.8 3.7 %shard_map.208 = (f32[1,256]{1,0:T(1,128)}, f32[1,256]{1,0:T(1,128)}, f32[1,64]{1,0:T(1,128)}, f32[1,64]{1,0:T(1,128)}, f32[2,784,128]{2,1,0:T(8,128)S(1)}, /*in...) custom-call(f32[224,128]{1,0:T(8,128)S(1)} %bitcast.56, f32[224,128]{1,0:T(8,128)S(1)} %bitcast.45, ...), custom_call_target="tpu_custom_call" | custom-call | tf_op jit(solution)/shard_map/pallas_call | solution.py:856
  59.5 10.3 %all_to_all.34 = bf16[32,10,2,128]{3,2,1,0:T(2,128)(2,1)S(1)} all-to-all(bf16[32,10,2,128]{3,2,1,0:T(2,128)(2,1)S(1)} %bitcast.57), channel_id=1, replica_groups=mesh['img'=8,'ha'=4] {'img','ha'}, dimensions={0} | all-to-all | bytes 327680 | tf_op jit(solution)/shard_map/all_to_all | solution.py:814
  69.7 1.0 %shard_map.209 = (f32[1,64]{1,0:T(1,128)}, f32[1,64]{1,0:T(1,128)}, bf16[2,2,784,256]{3,2,1,0:T(8,128)(2,1)S(1)}, bf16[576,128]{1,0:T(8,128)(2,1)}) custom-call(bf16[640,128]{1,0:T(8,128)(2,1)S(1)} %bitcast.50, f32[128,128]{1,0:T(8,128)S(1)} %bitcast.49, f32[128,128]{1,0:T(8,128)S(1)} %bitcast.52, f32[224,128]{1,0:T(8,128)S(1)} %bitcast.46, ...), custom_call_target="tpu_custom_call" | custom-call | tf_op jit(solution)/shard_map/pallas_call | solution.py:856
  70.8 2.6 %all-to-all-start.5 = ((bf16[32,9,2,128]{3,2,1,0:T(2,128)(2,1)}), bf16[32,9,2,128]{3,2,1,0:T(2,128)(2,1)S(1)}, u32[]{:S(2)}, u32[]{:S(2)}) async-start(bf16[32,9,2,128]{3,2,1,0:T(2,128)(2,1)} %bitcast.24), calls=%async_computation.5 | async-start | bytes 294912 | tf_op jit(solution)/shard_map/all_to_all | solution.py:814
  73.3 1.2 %copy.27 = bf16[4,14,56,256]{3,2,1,0:T(8,128)(2,1)} copy(bf16[4,14,56,256]{3,2,1,0:T(8,128)(2,1)S(1)} %bitcast.36) | data formatting | bytes 3211264
  74.5 7.3 %all-to-all-done.5 = bf16[32,9,2,128]{3,2,1,0:T(2,128)(2,1)S(1)} async-done(((bf16[32,9,2,128]{3,2,1,0:T(2,128)(2,1)}), bf16[32,9,2,128]{3,2,1,0:T(2,128)(2,1)S(1)}, u32[]{:S(2)}, u32[]{:S(2)}) %all-to-all-start.5) | async-done | bytes 147488 | tf_op jit(solution)/shard_map/all_to_all | solution.py:814
  81.8 0.8 shard_map.210
  (8 shorter events, 0.0 us)
Async XLA Ops:
  1.3 2.7 %copy-start = (bf16[4,14,56,256]{3,2,1,0:T(8,128)(2,1)S(1)}, bf16[4,14,56,256]{3,2,1,0:T(8,128)(2,1)}, u32[]{:S(2)}) copy-start(bf16[4,14,56,256]{3,2,1,0:T(8,128)(2,1)} %param.12) | copy-start | bytes 4816900
  2.7 18.0 %copy-start.2 = (bf16[3,3,64,64]{3,2,1,0:T(8,128)(2,1)S(1)}, bf16[3,3,64,64]{3,2,1,0:T(8,128)(2,1)}, u32[]{:S(2)}) copy-start(bf16[3,3,64,64]{3,2,1,0:T(8,128)(2,1)} %param.14) | copy-start | bytes 221188
  2.8 18.0 %copy-start.5 = (f32[64]{0:T(128)S(1)}, f32[64]{0:T(128)}, u32[]{:S(2)}) copy-start(f32[64]{0:T(128)} %param.16) | copy-start | bytes 772
  2.8 18.0 %copy-start.8 = (f32[64]{0:T(128)S(1)}, f32[64]{0:T(128)}, u32[]{:S(2)}) copy-start(f32[64]{0:T(128)} %param.17) | copy-start | bytes 772
  2.8 17.9 %collective-permute-start = (bf16[2,2,2,112,256]{4,3,2,1,0:T(8,128)(2,1)S(1)}, bf16[2,2,2,112,256]{4,3,2,1,0:T(8,128)(2,1)S(1)}, u32[]{:S(2)}, u32[]{:S(2)}) collective-permute-start(bf16[2,2,2,112,256]{4,3,2,1,0:T(8,128)(2,1)S(1)} %get-tuple-element.54), channel_id=1, source_target_pairs={{0,1},{1,0},{2,3},{3,2},{4,5},{5,4},{6,7},{7,6},{8,9},{9,8},{10,11... | collective-permute-start | bytes 1376264 | tf_op jit(solution)/shard_map/ppermute | solution.py:887
  3.3 17.4 %collective-permute-start.1 = (bf16[2,2,2,112,256]{4,3,2,1,0:T(8,128)(2,1)S(1)}, bf16[2,2,2,112,256]{4,3,2,1,0:T(8,128)(2,1)S(1)}, u32[]{:S(2)}, u32[]{:S(2)}) collective-permute-start(bf16[2,2,2,112,256]{4,3,2,1,0:T(8,128)(2,1)S(1)} %get-tuple-element.55), channel_id=1, source_target_pairs={{1,2},{2,1},{5,6},{6,5},{9,10},{10,9},{13,14},{14,13},{17,18},{18,... | collective-permute-start | bytes 1376264 | tf_op jit(solution)/shard_map/ppermute | solution.py:888
  20.7 11.1 %copy-start.3 = (bf16[64,256]{1,0:T(8,128)(2,1)S(1)}, bf16[64,256]{1,0:T(8,128)(2,1)}, u32[]{:S(2)}) copy-start(bf16[64,256]{1,0:T(8,128)(2,1)} %expander_ref.1) | copy-start | bytes 98308
  20.7 11.1 %copy-start.4 = (f32[64]{0:T(128)S(1)}, f32[64]{0:T(128)}, u32[]{:S(2)}) copy-start(f32[64]{0:T(128)} %param.18) | copy-start | bytes 772
  20.8 11.1 %copy-start.9 = (f32[64]{0:T(128)S(1)}, f32[64]{0:T(128)}, u32[]{:S(2)}) copy-start(f32[64]{0:T(128)} %param.19) | copy-start | bytes 772
  20.8 22.3 %copy-start.1 = (bf16[4,14,56,256]{3,2,1,0:T(8,128)(2,1)S(1)}, bf16[4,14,56,256]{3,2,1,0:T(8,128)(2,1)}, u32[]{:S(2)}) copy-start(bf16[4,14,56,256]{3,2,1,0:T(8,128)(2,1)} %param.22) | copy-start | bytes 4816900
  20.8 22.3 %copy-start.6 = (f32[256]{0:T(256)S(1)}, f32[256]{0:T(256)}, u32[]{:S(2)}) copy-start(f32[256]{0:T(256)} %param.20) | copy-start | bytes 3076
  20.8 22.3 %copy-start.7 = (f32[256]{0:T(256)S(1)}, f32[256]{0:T(256)}, u32[]{:S(2)}) copy-start(f32[256]{0:T(256)} %param.21) | copy-start | bytes 3076
  70.8 11.0 %all-to-all-start.5 = ((bf16[32,9,2,128]{3,2,1,0:T(2,128)(2,1)}), bf16[32,9,2,128]{3,2,1,0:T(2,128)(2,1)S(1)}, u32[]{:S(2)}, u32[]{:S(2)}) async-start(bf16[32,9,2,128]{3,2,1,0:T(2,128)(2,1)} %bitcast.24), calls=%async_computation.5 | async-start | bytes 294912 | tf_op jit(solution)/shard_map/all_to_all | solution.py:814
